TPU v7x, 32 devices: a whole 2x2x4 slice. The times are simulated.
32 devices in a mesh: dev: 32 (over z, y, x, core).
Axes of the slice: x: 2, y: 2, z: 4, core: 2. Of those that a mesh axis runs over, the one named last changes fastest.
Arguments:
- embeddings: bfloat16 [8192, 1024], P('dev'), may hold values from -6 to 6
- cluster_id: int32 [8192], P('dev'), may hold values from 0 to 15, as said below
- requests: int32 [1024], P('dev'), may hold values from -1 to 1, as said below
- pair_left: int32 [12288], P('dev'), may hold values from 0 to 31, as said below
- pair_right: int32 [12288], P('dev'), may hold values from 0 to 31, as said below
Outputs:
- best: float32 [8192], P('dev')
Inputs may be any that keep to these rules, and one draw needn't show every extreme that they name: Rows are sorted by cluster: cluster_id never falls along the rows, and every cluster has rows. Every slot that some task of device d names has a block (requests at least 0 there); a device's tasks name slots of at most 32 consecutive owners. pair_left <= pair_right for every task; no device lists one slot pair twice. `pair_right`: see pair_left.
All inputs are finite; a program needn't handle non-finite values.
Results may differ from a plain program's by a relative error of at most 0.00086.
Values may be sent and summed in bfloat16 or wider, within the bound.
No kernel may reach another device: no remote copies, remote signals or barrier semaphores. Data moves between devices by JAX's collectives and lax.ppermute only.
A program may use at most 192 MiB of HBM per device.

v0:
```python
import functools

import jax
import jax.numpy as jnp
from jax import lax
from jax.experimental import pallas as pl
from jax.experimental.pallas import tpu as pltpu
from jax.sharding import PartitionSpec as P

BLOCK = 128
CLUSTERS = 16
PLANE = 8
JOIN_COST = 10_000_000_000
AXIS = "dev"
LABEL_ROWS = 16
VMEM_TILES = 8 * 1024 * 1024


def normalise_kernel(x_hbm, cluster_hbm, unit_ref, x_ref, cluster_ref, sems):
    copies = [
        pltpu.make_async_copy(x_hbm, x_ref, sems.at[0]),
        pltpu.make_async_copy(cluster_hbm, cluster_ref, sems.at[1]),
    ]
    for copy in copies:
        copy.start()
    rows, depth = x_ref.shape
    unit_ref[rows:] = jnp.zeros((LABEL_ROWS, depth), jnp.bfloat16)
    copies[1].wait()
    label = (cluster_ref[...] + 1).astype(jnp.bfloat16)
    unit_ref[rows:, :rows] = jnp.broadcast_to(label, (LABEL_ROWS, rows))
    copies[0].wait()
    values = x_ref[...].astype(jnp.float32)
    norm = lax.rsqrt(jnp.sum(values * values, axis=-1, keepdims=True) + 1e-06)
    unit_ref[:rows] = (values * norm).astype(jnp.bfloat16)


def normalise(x, cluster_id):
    rows, depth = x.shape
    return pl.pallas_call(
        normalise_kernel,
        name="normalise",
        in_specs=[pl.BlockSpec(memory_space=pltpu.HBM)] * 2,
        out_shape=jax.ShapeDtypeStruct((rows + LABEL_ROWS, depth), jnp.bfloat16),
        scratch_shapes=[
            pltpu.VMEM((rows, depth), x.dtype),
            pltpu.VMEM((1, rows), jnp.int32),
            pltpu.SemaphoreType.DMA((2,)),
        ],
        compiler_params=pltpu.CompilerParams(vmem_limit_bytes=60 * 1024 * 1024),
    )(x, cluster_id.reshape(1, rows))


def message_kernel(n, left_ref, right_ref, request_ref, cluster_ref, out_ref):
    def dot(a, b):
        return lax.dot_general(a, b, (((1,), (1,)), ((), ())), preferred_element_type=jnp.float32)

    def hot(count, ref):
        index = lax.broadcasted_iota(jnp.int32, (count, ref.shape[1]), 0)
        return (index == ref[...]).astype(jnp.float32).astype(jnp.bfloat16)

    left, right, cluster = hot(n, left_ref), hot(n, right_ref), hot(CLUSTERS, cluster_ref)
    out_ref[...] = jnp.zeros(out_ref.shape, jnp.float32)
    out_ref[:, 0, :n] = dot(left, right) + dot(right, left)
    out_ref[:, 0, n : 2 * n] = jnp.broadcast_to(request_ref[...].astype(jnp.float32), (n, n))
    counts = dot(jnp.ones((n, cluster.shape[1]), jnp.bfloat16), cluster)
    out_ref[:, 0, 2 * n : 2 * n + CLUSTERS] = counts


def message_of(requests, pair_left, pair_right, cluster_id):
    n = requests.shape[0]
    width = -(-(2 * n + CLUSTERS) // BLOCK) * BLOCK
    return pl.pallas_call(
        functools.partial(message_kernel, n),
        name="message",
        out_shape=jax.ShapeDtypeStruct((n, 1, width), jnp.float32),
        compiler_params=pltpu.CompilerParams(vmem_limit_bytes=4 * 1024 * 1024),
    )(pair_left.reshape(1, -1), pair_right.reshape(1, -1), requests.reshape(1, -1), cluster_id.reshape(1, -1))


def cover_kernel(blk_dev, rows, offset_ref, heard_ref, cap_ref, span_ref):
    n = heard_ref.shape[0]
    me = lax.axis_index(AXIS)

    def iota(shape, dimension):
        return lax.broadcasted_iota(jnp.int32, shape, dimension)

    def hot(mask):
        return mask.astype(jnp.float32)

    listed = heard_ref[:, 0, :n] > 0
    requests = heard_ref[:, 0, n : 2 * n]
    own = jnp.sum(jnp.where(iota((n, n), 1) == me, requests, 0.0), axis=1, keepdims=True)
    owns = hot(own == (iota((n, rows), 1) // BLOCK).astype(jnp.float32)).astype(jnp.bfloat16)
    height = cap_ref.shape[1]
    at = iota((4 * height, n), 0)
    source, at = at // height, at % height
    near = at < 8
    at = jnp.where(near, at, at - 8)
    part, block = at // blk_dev, at % blk_dev
    step = jnp.where(near, 0, jnp.where(part < 2, offset_ref[0], -offset_ref[0]))
    device = ((2 * source + part % 2) ^ me) + step * PLANE
    device = jnp.where(near & (part >= 2), -1, device)
    total = jnp.zeros((4 * height, rows), jnp.float32)
    for b in range(blk_dev):
        asked = hot(listed & (requests == b)).T.astype(jnp.bfloat16)
        count = jnp.dot(asked, owns, preferred_element_type=jnp.float32)
        pick = hot((iota((4 * height, n), 1) == device) & (block == b)).astype(jnp.bfloat16)
        total += jnp.dot(pick, hot(count > 0).astype(jnp.bfloat16), preferred_element_type=jnp.float32)
    cap_ref[...] = jnp.where(total > 0, jnp.inf, -1.0).reshape(cap_ref.shape)
    present = heard_ref[:, 0, 2 * n : 2 * n + CLUSTERS] > 0
    plane = (iota((n, CLUSTERS), 0) // PLANE).astype(jnp.float32)
    first = jnp.min(jnp.where(present, plane, float(n)), axis=0, keepdims=True)
    last = jnp.max(jnp.where(present, plane, -1.0), axis=0, keepdims=True)
    span_ref[0] = jnp.max(last - first).astype(jnp.int32)


def cover(heard, offset, blk_dev, rows):
    cap, span = pl.pallas_call(
        functools.partial(cover_kernel, blk_dev, rows),
        name="cover",
        in_specs=[pl.BlockSpec(memory_space=pltpu.SMEM), pl.BlockSpec(memory_space=pltpu.VMEM)],
        out_specs=[pl.BlockSpec(memory_space=pltpu.VMEM), pl.BlockSpec(memory_space=pltpu.SMEM)],
        out_shape=[
            jax.ShapeDtypeStruct((4, 8 + 4 * blk_dev, rows), jnp.float32),
            jax.ShapeDtypeStruct((1,), jnp.int32),
        ],
        compiler_params=pltpu.CompilerParams(vmem_limit_bytes=8 * 1024 * 1024),
    )(jnp.asarray(offset, jnp.int32).reshape(1), heard)
    return cap, span[0]


def halves_kernel(x_ref, y_ref, first_ref, second_ref):
    first_ref[...] = x_ref[: first_ref.shape[0]]
    second_ref[...] = y_ref[first_ref.shape[0] :]


def halves(x, y):
    half = (x.shape[0] - LABEL_ROWS) // 2
    return pl.pallas_call(
        halves_kernel,
        name="halves",
        out_shape=[
            jax.ShapeDtypeStruct((half, x.shape[1]), x.dtype),
            jax.ShapeDtypeStruct((half + LABEL_ROWS, x.shape[1]), x.dtype),
        ],
        compiler_params=pltpu.CompilerParams(vmem_limit_bytes=4 * 1024 * 1024),
        cost_estimate=pl.CostEstimate(flops=0, bytes_accessed=x.size * 4, transcendentals=0),
    )(x, y)


def arrived_kernel(first_ref, second_ref, token_ref):
    del first_ref, second_ref
    token_ref[...] = jnp.zeros(token_ref.shape, jnp.float32)


def arrived(pieces):
    return pl.pallas_call(
        arrived_kernel,
        name="arrived",
        in_specs=[pl.BlockSpec(memory_space=pl.ANY)] * 2,
        out_shape=jax.ShapeDtypeStruct((8, 128), jnp.float32),
        compiler_params=pltpu.CompilerParams(vmem_limit_bytes=1024 * 1024),
        cost_estimate=pl.CostEstimate(flops=JOIN_COST, bytes_accessed=4096, transcendentals=0),
    )(*pieces)


def tile_kernel(counts, n_right, places, rows, own_first, n_before, n_token, *refs):
    parts, copies = [], []
    n_operands = sum(max(count, 1) for count in counts)
    tail = refs[n_operands + n_before + n_token :]
    outs, scratch = tail[:n_right], tail[n_right:]
    operands, before = list(refs[:n_operands]), refs[n_operands : n_operands + n_before]
    sem = 0
    for count in counts:
        here, operands = operands[: max(count, 1)], operands[max(count, 1) :]
        if not count:
            parts.append(here[0])
            copies.append([])
            continue
        part, top, own = scratch[sum(1 for c in copies if c)], 0, []
        for piece in here:
            own.append(pltpu.make_async_copy(piece, part.at[pl.ds(top, piece.shape[0])], scratch[-1].at[sem]))
            own[-1].start()
            top, sem = top + piece.shape[0], sem + 1
        parts.append(part)
        copies.append(own)
    for r, out in enumerate(outs):
        out[...] = jnp.full(out.shape, -1.0, jnp.float32)
        if r < n_before:
            out[: before[r].shape[0]] = before[r][...]
    blocks = rows // BLOCK
    labels = {}

    def labels_of(k):
        if k not in labels:
            for copy in copies[k]:
                copy.wait()
            label = parts[k][rows:, :rows].astype(jnp.float32)[:1]
            labels[k] = label, jnp.min(label), jnp.max(label)
        return labels[k]

    def tile(r, c):
        sims = lax.dot_general(
            parts[n_right + c][:rows],
            parts[r][:rows],
            (((1,), (1,)), ((), ())),
            preferred_element_type=jnp.float32,
        )
        for b in range(blocks):
            at = slice(b * BLOCK, (b + 1) * BLOCK)
            label = jnp.broadcast_to(labels[n_right + c][0][:, at], (BLOCK, BLOCK)).T
            label = jnp.concatenate([label] * blocks, axis=1)
            same = label == labels[r][0]
            part = sims[at]
            if own_first and c == 0 and r == 0:
                index = lax.broadcasted_iota(jnp.int32, part.shape, 0) + b * BLOCK
                same &= index != lax.broadcasted_iota(jnp.int32, part.shape, 1)
            part = jnp.where(same, part, -1.0)
            row = places[c] + b
            outs[r][row : row + 1, :] = jnp.max(part, axis=0, keepdims=True)

    todo = [
        (r, c)
        for c in range(len(places))
        for r in range(n_right)
        if r >= n_before or places[c] >= before[r].shape[0]
    ]
    for r, c in sorted(todo, key=lambda rc: (len(copies[n_right + rc[1]]), len(copies[rc[0]]))):
        right, left = labels_of(r), labels_of(n_right + c)
        pl.when((left[1] <= right[2]) & (right[1] <= left[2]))(functools.partial(tile, r, c))


def tiles(name, rights, lefts, places, own_first, before=(), token=None, flops=None):
    parts = list(rights) + list(lefts)
    counts = tuple(len(part) if isinstance(part, list) else 0 for part in parts)
    operands = [piece for part in parts for piece in (part if isinstance(part, list) else [part])]
    height_in, depth = operands[0].shape
    rows = height_in - LABEL_ROWS
    height = -(-(places[-1] + rows // BLOCK) // 8) * 8
    if flops is None:
        flops = 2 * len(rights) * len(lefts) * rows * rows * depth
    vmem, anywhere = pl.BlockSpec(memory_space=pltpu.VMEM), pl.BlockSpec(memory_space=pl.ANY)
    specs = [spec for count in counts for spec in ([anywhere] * count if count else [vmem])]
    extra = list(before) + ([] if token is None else [token])
    scratch = [pltpu.VMEM((height_in, depth), jnp.bfloat16) for count in counts if count]
    if scratch:
        scratch.append(pltpu.SemaphoreType.DMA((sum(counts),)))
    return pl.pallas_call(
        functools.partial(tile_kernel, counts, len(rights), tuple(places), rows, own_first, len(before), len(extra) - len(before)),
        name=name,
        in_specs=specs + [vmem] * len(extra),
        out_specs=[vmem] * len(rights),
        out_shape=[jax.ShapeDtypeStruct((height, rows), jnp.float32)] * len(rights),
        scratch_shapes=scratch,
        compiler_params=pltpu.CompilerParams(vmem_limit_bytes=VMEM_TILES),
        cost_estimate=pl.CostEstimate(
            flops=flops, bytes_accessed=2 * len(operands) * rows * depth, transcendentals=0
        ),
    )(*operands, *extra)


def local(embeddings, cluster_id, requests, pair_left, pair_right):
    n = lax.axis_size(AXIS)
    rows = embeddings.shape[0]
    blk_dev = rows // BLOCK

    def swap(x, bit):
        return lax.ppermute(x, AXIS, [(i, i ^ bit) for i in range(n)])

    def from_above(x):
        return lax.ppermute(x, AXIS, [(i + PLANE, i) for i in range(n - PLANE)])

    def from_below(x):
        return lax.ppermute(x, AXIS, [(i, i + PLANE) for i in range(n - PLANE)])

    def owners_best(parts, cap):
        mine, for_x, for_y, for_across = parts
        returned = jnp.stack([mine, swap(for_x, 2), swap(for_y, 4), swap(for_across, 6)])
        return jnp.maximum(jnp.max(jnp.minimum(returned, cap), axis=(0, 1)), -1.0)

    unit = normalise(embeddings, cluster_id)
    along_x, along_y = swap(unit, 2), swap(unit, 4)
    above, below = from_above(unit), from_below(unit)
    twin = swap(unit, 1)
    message = message_of(requests, pair_left, pair_right, cluster_id)
    along_x, message = lax.optimization_barrier((along_x, message))
    first, second = halves(along_x, along_y)
    pieces = [swap(first, 4), swap(second, 2)]
    along_x, first = lax.optimization_barrier((along_x, first))
    above_twin, below_twin = swap(above, 1), swap(below, 1)

    heard = lax.all_to_all(message, AXIS, split_axis=0, concat_axis=0, tiled=True)

    plane_places = [0, blk_dev]
    next_places = [8 + blk_dev * k for k in range(4)]
    lefts = [[above], above_twin, [below], below_twin]
    near_rights = [unit, along_x, along_y]
    plane_parts = tiles("plane_tiles", near_rights, [unit, twin], plane_places, True)
    token = arrived(pieces)
    parts = tiles(
        "all_tiles",
        near_rights + [pieces],
        [unit, twin] + lefts,
        plane_places + next_places,
        False,
        plane_parts,
        token,
        flops=0,
    )
    cap, span = cover(heard, 1, blk_dev, rows)
    best = owners_best(parts, cap)

    def further(best):
        def body(carry):
            offset, best, above, below = carry
            above, below = from_above(above), from_below(below)
            lefts = [above, swap(above, 1), below, swap(below, 1)]
            parts = tiles(
                "further_tiles",
                near_rights + [pieces],
                lefts,
                [blk_dev * k for k in range(4)],
                False,
            )
            cap, _ = cover(heard, offset, blk_dev, rows)
            best = jnp.maximum(best, owners_best(parts, cap[:, 8:]))
            return offset + 1, best, above, below

        return lax.while_loop(lambda carry: carry[0] <= span, body, (jnp.int32(2), best, above, below))[1]

    return lax.cond(span >= 2, further, lambda best: best, best)


def solution(mesh):
    in_specs = (P(AXIS, None), P(AXIS), P(AXIS), P(AXIS), P(AXIS))
    return jax.shard_map(local, mesh=mesh, in_specs=in_specs, out_specs=P(AXIS), check_vma=False)
```

profile of v0, /device:TPU:0, one launch (start us, length us, event | category | flops | bytes accessed | tf_op | source)
XLA Modules:
  0.0 39.5 jit_solution(6880720470421528549)
XLA Ops:
  0.0 1.3 %normalise.1.refs_0_.refs_3_.refs_5_ = bf16[272,1024]{1,0:T(8,128)(2,1)S(1)} custom-call(bf16[256,1024]{1,0:T(8,128)(2,1)} %x_hbm.1, s32[1,256]{1,0:T(1,128)} %bitcast.24), custom_call_target="tpu_custom_call" | custom-call | tf_op jit(solution)/shard_map/normalise/pallas_call | solution.py:39
  1.3 0.0 copy-start.4
  1.3 3.0 %collective-permute-start.7 = (bf16[272,1024]{1,0:T(8,128)(2,1)S(1)}, bf16[272,1024]{1,0:T(8,128)(2,1)S(1)}, u32[]{:S(2)}, u32[]{:S(2)}) collective-permute-start(bf16[272,1024]{1,0:T(8,128)(2,1)S(1)} %normalise.1.refs_0_.refs_3_.refs_5_), channel_id=1, source_target_pairs={{0,2},{1,3},{2,0},{3,1},{4,6},{5,7},{6,4},{7,5},{8,10},{9,11},{10,... | collective-permute-start | bytes 1671176 | tf_op jit(solution)/shard_map/ppermute | solution.py:268
  4.3 1.5 %collective-permute-start.8 = (bf16[272,1024]{1,0:T(8,128)(2,1)S(1)}, bf16[272,1024]{1,0:T(8,128)(2,1)S(1)}, u32[]{:S(2)}, u32[]{:S(2)}) collective-permute-start(bf16[272,1024]{1,0:T(8,128)(2,1)S(1)} %normalise.1.refs_0_.refs_3_.refs_5_), channel_id=1, source_target_pairs={{0,4},{1,5},{2,6},{3,7},{4,0},{5,1},{6,2},{7,3},{8,12},{9,13},{10,... | collective-permute-start | bytes 1671176 | tf_op jit(solution)/shard_map/ppermute | solution.py:268
  5.8 1.3 %collective-permute-start.12 = (bf16[272,1024]{1,0:T(8,128)(2,1)S(1)}, bf16[272,1024]{1,0:T(8,128)(2,1)S(1)}, u32[]{:S(2)}, u32[]{:S(2)}) collective-permute-start(bf16[272,1024]{1,0:T(8,128)(2,1)S(1)} %normalise.1.refs_0_.refs_3_.refs_5_), channel_id=1, source_target_pairs={{8,0},{9,1},{10,2},{11,3},{12,4},{13,5},{14,6},{15,7},{16,8},{17,9... | collective-permute-start | bytes 1671176 | tf_op jit(solution)/shard_map/ppermute | solution.py:271
  7.1 5.4 %collective-permute-start.14 = (bf16[272,1024]{1,0:T(8,128)(2,1)S(1)}, bf16[272,1024]{1,0:T(8,128)(2,1)}, u32[]{:S(2)}, u32[]{:S(2)}) collective-permute-start(bf16[272,1024]{1,0:T(8,128)(2,1)S(1)} %normalise.1.refs_0_.refs_3_.refs_5_), channel_id=1, source_target_pairs={{0,8},{1,9},{2,10},{3,11},{4,12},{5,13},{6,14},{7,15},{8,16},{9,17... | collective-permute-start | bytes 1671176 | tf_op jit(solution)/shard_map/ppermute | solution.py:274
  12.5 0.0 copy-start
  12.5 0.0 copy-start.1
  12.5 0.7 %copy-done = s32[256]{0:T(256)S(1)} copy-done((s32[256]{0:T(256)S(1)}, s32[256]{0:T(256)}, u32[]{:S(2)}) %copy-start) | copy-done | bytes 1048
  13.2 0.9 %message.1 = f32[32,1,128]{2,1,0:T(1,128)} custom-call(s32[1,384]{1,0:T(1,128)S(1)} %reshape.17.left_ref, s32[1,384]{1,0:T(1,128)S(1)} %reshape.18.right_ref, s32[1,32]{1,0:T(1,128)S(1)} %bitcast.26, s32[1,256]{1,0:T(1,128)S(1)} %bitcast.25), custom_call_target="tpu_custom_call" | custom-call | tf_op jit(solution)/shard_map/message/pallas_call | solution.py:72
  14.0 2.9 %collective-permute-done.7.x_ref.refs_1_ = bf16[272,1024]{1,0:T(8,128)(2,1)S(1)} collective-permute-done((bf16[272,1024]{1,0:T(8,128)(2,1)S(1)}, bf16[272,1024]{1,0:T(8,128)(2,1)S(1)}, u32[]{:S(2)}, u32[]{:S(2)}) %collective-permute-start.7) | collective-permute-done | bytes 557088 | tf_op jit(solution)/shard_map/ppermute | solution.py:268
  16.9 1.5 %collective-permute-done.8.y_ref.refs_2_ = bf16[272,1024]{1,0:T(8,128)(2,1)S(1)} collective-permute-done((bf16[272,1024]{1,0:T(8,128)(2,1)S(1)}, bf16[272,1024]{1,0:T(8,128)(2,1)S(1)}, u32[]{:S(2)}, u32[]{:S(2)}) %collective-permute-start.8) | collective-permute-done | bytes 557088 | tf_op jit(solution)/shard_map/ppermute | solution.py:268
  18.4 0.4 %collective-permute-start.10 = (bf16[144,1024]{1,0:T(8,128)(2,1)S(1)}, bf16[144,1024]{1,0:T(8,128)(2,1)}, u32[]{:S(2)}, u32[]{:S(2)}) collective-permute-start(bf16[144,1024]{1,0:T(8,128)(2,1)S(1)} %get-tuple-element.121), channel_id=1, source_target_pairs={{0,2},{1,3},{2,0},{3,1},{4,6},{5,7},{6,4},{7,5},{8,10},{9,11},{10,... | collective-permute-start | bytes 884744 | tf_op jit(solution)/shard_map/ppermute | solution.py:268
  18.8 1.7 %collective-permute-start.9 = (bf16[128,1024]{1,0:T(8,128)(2,1)S(1)}, bf16[128,1024]{1,0:T(8,128)(2,1)}, u32[]{:S(2)}, u32[]{:S(2)}) collective-permute-start(bf16[128,1024]{1,0:T(8,128)(2,1)S(1)} %get-tuple-element.119), channel_id=1, source_target_pairs={{0,4},{1,5},{2,6},{3,7},{4,0},{5,1},{6,2},{7,3},{8,12},{9,13},{10,... | collective-permute-start | bytes 786440 | tf_op jit(solution)/shard_map/ppermute | solution.py:268
  20.5 4.9 %all-to-all-start = ((f32[32,1,128]{2,1,0:T(1,128)}), f32[32,1,128]{2,1,0:T(1,128)S(1)}, u32[]{:S(2)}, u32[]{:S(2)}) async-start(f32[32,1,128]{2,1,0:T(1,128)} %message.1), calls=%async_computation | async-start | bytes 32768 | tf_op jit(solution)/shard_map/all_to_all | solution.py:292
  25.4 0.3 collective-permute-start.13
  25.8 0.0 collective-permute-done.14.refs_9_
  25.8 0.3 collective-permute-start.15
  26.0 0.0 collective-permute-done.11.refs_4_.refs_6_
  26.0 2.6 %plane_tiles.1 = (f32[8,256]{1,0:T(8,128)S(1)}, f32[8,256]{1,0:T(8,128)S(1)}, f32[8,256]{1,0:T(8,128)S(1)}) custom-call(bf16[272,1024]{1,0:T(8,128)(2,1)S(1)} %normalise.1.refs_0_.refs_3_.refs_5_, bf16[272,1024]{1,0:T(8,128)(2,1)S(1)} %collective-permute-done.7.x_ref.refs_1_, bf16[272,1024]{1,0:T(8,128)(2,1)S(1)} %collective-permute-done.8.y_ref.refs_2_, ...), custom_call_target="tpu_custom_call" | custom-call | flops 805306368 | bytes 2621440 | tf_op jit(solution)/shard_map/plane_tiles/pallas_call | solution.py:248
  28.6 0.0 collective-permute-done.9.first_ref.refs_3_
  28.6 0.0 collective-permute-done.10.second_ref.refs_4_
  28.7 0.0 collective-permute-done.13.refs_8_
  28.7 0.0 collective-permute-done.15.refs_10_
  28.7 4.7 %all_tiles.1 = (f32[16,256]{1,0:T(8,128)S(1)}, f32[16,256]{1,0:T(8,128)S(1)}, f32[16,256]{1,0:T(8,128)S(1)}, f32[16,256]{1,0:T(8,128)S(1)}) custom-call(bf16[272,1024]{1,0:T(8,128)(2,1)S(1)} %normalise.1.refs_0_.refs_3_.refs_5_, bf16[272,1024]{1,0:T(8,128)(2,1)S(1)} %collective-permute-done.7.x_ref.refs_1_, ...), custom_call_target="tpu_custom_call" | custom-call | bytes 5767168 | tf_op jit(solution)/shard_map/all_tiles/pallas_call | solution.py:248
  33.4 0.1 collective-permute-start.17
  33.5 0.9 %collective-permute-start.18 = (f32[16,256]{1,0:T(8,128)S(1)}, f32[16,256]{1,0:T(8,128)S(1)}, u32[]{:S(2)}, u32[]{:S(2)}) collective-permute-start(f32[16,256]{1,0:T(8,128)S(1)} %get-tuple-element.128), channel_id=1, source_target_pairs={{0,6},{1,7},{2,4},{3,5},{4,2},{5,3},{6,0},{7,1},{8,14},{9,15},{10,... | collective-permute-start | bytes 49160 | tf_op jit(solution)/shard_map/ppermute | solution.py:268
  34.3 2.6 %collective-permute-start.16 = (f32[16,256]{1,0:T(8,128)S(1)}, f32[16,256]{1,0:T(8,128)S(1)}, u32[]{:S(2)}, u32[]{:S(2)}) collective-permute-start(f32[16,256]{1,0:T(8,128)S(1)} %get-tuple-element.126), channel_id=1, source_target_pairs={{0,2},{1,3},{2,0},{3,1},{4,6},{5,7},{6,4},{7,5},{8,10},{9,11},{10,... | collective-permute-start | bytes 49160 | tf_op jit(solution)/shard_map/ppermute | solution.py:268
  37.0 0.9 %cover.2 = (f32[4,16,256]{2,1,0:T(8,128)S(1)}, s32[1]{0:T(128)}) custom-call(s32[1]{0:T(128)} %constant.4.clone.1.offset_ref, f32[32,1,128]{2,1,0:T(1,128)S(1)} %all-to-all-done.heard_ref), custom_call_target="tpu_custom_call" | custom-call | tf_op jit(solution)/shard_map/cover/pallas_call | solution.py:118
  38.5 0.3 collective-permute-done.16
  38.9 0.0 copy-start.2
  38.9 0.6 %copy-done.2 = f32[256]{0:T(256)} copy-done((f32[256]{0:T(256)}, f32[256]{0:T(256)S(1)}, u32[]{:S(2)}) %copy-start.2) | copy-done | bytes 1048
  (16 shorter events, 0.1 us)
Async XLA Ops:
  0.0 12.5 %copy-start.3 = (s32[384]{0:T(512)S(1)}, s32[384]{0:T(512)}, u32[]{:S(2)}) copy-start(s32[384]{0:T(512)} %param.12) | copy-start | bytes 4612
  1.3 11.2 %copy-start.4 = (s32[384]{0:T(512)S(1)}, s32[384]{0:T(512)}, u32[]{:S(2)}) copy-start(s32[384]{0:T(512)} %param.13) | copy-start | bytes 4612
  1.3 15.6 %collective-permute-start.7 = (bf16[272,1024]{1,0:T(8,128)(2,1)S(1)}, bf16[272,1024]{1,0:T(8,128)(2,1)S(1)}, u32[]{:S(2)}, u32[]{:S(2)}) collective-permute-start(bf16[272,1024]{1,0:T(8,128)(2,1)S(1)} %normalise.1.refs_0_.refs_3_.refs_5_), channel_id=1, source_target_pairs={{0,2},{1,3},{2,0},{3,1},{4,6},{5,7},{6,4},{7,5},{8,10},{9,11},{10,... | collective-permute-start | bytes 1671176 | tf_op jit(solution)/shard_map/ppermute | solution.py:268
  4.3 14.1 %collective-permute-start.8 = (bf16[272,1024]{1,0:T(8,128)(2,1)S(1)}, bf16[272,1024]{1,0:T(8,128)(2,1)S(1)}, u32[]{:S(2)}, u32[]{:S(2)}) collective-permute-start(bf16[272,1024]{1,0:T(8,128)(2,1)S(1)} %normalise.1.refs_0_.refs_3_.refs_5_), channel_id=1, source_target_pairs={{0,4},{1,5},{2,6},{3,7},{4,0},{5,1},{6,2},{7,3},{8,12},{9,13},{10,... | collective-permute-start | bytes 1671176 | tf_op jit(solution)/shard_map/ppermute | solution.py:268
  5.8 19.6 %collective-permute-start.12 = (bf16[272,1024]{1,0:T(8,128)(2,1)S(1)}, bf16[272,1024]{1,0:T(8,128)(2,1)S(1)}, u32[]{:S(2)}, u32[]{:S(2)}) collective-permute-start(bf16[272,1024]{1,0:T(8,128)(2,1)S(1)} %normalise.1.refs_0_.refs_3_.refs_5_), channel_id=1, source_target_pairs={{8,0},{9,1},{10,2},{11,3},{12,4},{13,5},{14,6},{15,7},{16,8},{17,9... | collective-permute-start | bytes 1671176 | tf_op jit(solution)/shard_map/ppermute | solution.py:271
  7.1 18.7 %collective-permute-start.14 = (bf16[272,1024]{1,0:T(8,128)(2,1)S(1)}, bf16[272,1024]{1,0:T(8,128)(2,1)}, u32[]{:S(2)}, u32[]{:S(2)}) collective-permute-start(bf16[272,1024]{1,0:T(8,128)(2,1)S(1)} %normalise.1.refs_0_.refs_3_.refs_5_), channel_id=1, source_target_pairs={{0,8},{1,9},{2,10},{3,11},{4,12},{5,13},{6,14},{7,15},{8,16},{9,17... | collective-permute-start | bytes 1671176 | tf_op jit(solution)/shard_map/ppermute | solution.py:274
  12.5 13.6 %collective-permute-start.11 = (bf16[272,1024]{1,0:T(8,128)(2,1)S(1)}, bf16[272,1024]{1,0:T(8,128)(2,1)S(1)}, u32[]{:S(2)}, u32[]{:S(2)}) collective-permute-start(bf16[272,1024]{1,0:T(8,128)(2,1)S(1)} %normalise.1.refs_0_.refs_3_.refs_5_), channel_id=1, source_target_pairs={{0,1},{1,0},{2,3},{3,2},{4,5},{5,4},{6,7},{7,6},{8,9},{9,8},{10,11... | collective-permute-start | bytes 1671176 | tf_op jit(solution)/shard_map/ppermute | solution.py:268
  12.5 0.7 %copy-start = (s32[256]{0:T(256)S(1)}, s32[256]{0:T(256)}, u32[]{:S(2)}) copy-start(s32[256]{0:T(256)} %param.10) | copy-start | bytes 3076
  12.5 0.7 %copy-start.1 = (s32[32]{0:T(128)S(1)}, s32[32]{0:T(128)}, u32[]{:S(2)}) copy-start(s32[32]{0:T(128)} %param.11) | copy-start | bytes 388
  18.4 10.2 %collective-permute-start.10 = (bf16[144,1024]{1,0:T(8,128)(2,1)S(1)}, bf16[144,1024]{1,0:T(8,128)(2,1)}, u32[]{:S(2)}, u32[]{:S(2)}) collective-permute-start(bf16[144,1024]{1,0:T(8,128)(2,1)S(1)} %get-tuple-element.121), channel_id=1, source_target_pairs={{0,2},{1,3},{2,0},{3,1},{4,6},{5,7},{6,4},{7,5},{8,10},{9,11},{10,... | collective-permute-start | bytes 884744 | tf_op jit(solution)/shard_map/ppermute | solution.py:268
  18.8 9.8 %collective-permute-start.9 = (bf16[128,1024]{1,0:T(8,128)(2,1)S(1)}, bf16[128,1024]{1,0:T(8,128)(2,1)}, u32[]{:S(2)}, u32[]{:S(2)}) collective-permute-start(bf16[128,1024]{1,0:T(8,128)(2,1)S(1)} %get-tuple-element.119), channel_id=1, source_target_pairs={{0,4},{1,5},{2,6},{3,7},{4,0},{5,1},{6,2},{7,3},{8,12},{9,13},{10,... | collective-permute-start | bytes 786440 | tf_op jit(solution)/shard_map/ppermute | solution.py:268
  20.5 16.4 %all-to-all-start = ((f32[32,1,128]{2,1,0:T(1,128)}), f32[32,1,128]{2,1,0:T(1,128)S(1)}, u32[]{:S(2)}, u32[]{:S(2)}) async-start(f32[32,1,128]{2,1,0:T(1,128)} %message.1), calls=%async_computation | async-start | bytes 32768 | tf_op jit(solution)/shard_map/all_to_all | solution.py:292
  25.4 3.2 %collective-permute-start.13 = (bf16[272,1024]{1,0:T(8,128)(2,1)S(1)}, bf16[272,1024]{1,0:T(8,128)(2,1)S(1)}, u32[]{:S(2)}, u32[]{:S(2)}) collective-permute-start(bf16[272,1024]{1,0:T(8,128)(2,1)S(1)} %collective-permute-done.12.refs_7_), channel_id=1, source_target_pairs={{0,1},{1,0},{2,3},{3,2},{4,5},{5,4},{6,7},{7,6},{8,9},{9,8},{10,11... | collective-permute-start | bytes 1671176 | tf_op jit(solution)/shard_map/ppermute | solution.py:268
  25.8 2.9 %collective-permute-start.15 = (bf16[272,1024]{1,0:T(8,128)(2,1)}, bf16[272,1024]{1,0:T(8,128)(2,1)S(1)}, u32[]{:S(2)}, u32[]{:S(2)}) collective-permute-start(bf16[272,1024]{1,0:T(8,128)(2,1)} %collective-permute-done.14.refs_9_), channel_id=1, source_target_pairs={{0,1},{1,0},{2,3},{3,2},{4,5},{5,4},{6,7},{7,6},{8,9},{9,8},{10,11... | collective-permute-start | bytes 1671176 | tf_op jit(solution)/shard_map/ppermute | solution.py:268
  33.4 5.1 %collective-permute-start.17 = (f32[16,256]{1,0:T(8,128)S(1)}, f32[16,256]{1,0:T(8,128)S(1)}, u32[]{:S(2)}, u32[]{:S(2)}) collective-permute-start(f32[16,256]{1,0:T(8,128)S(1)} %get-tuple-element.127), channel_id=1, source_target_pairs={{0,4},{1,5},{2,6},{3,7},{4,0},{5,1},{6,2},{7,3},{8,12},{9,13},{10,... | collective-permute-start | bytes 49160 | tf_op jit(solution)/shard_map/ppermute | solution.py:268
  33.5 5.0 %collective-permute-start.18 = (f32[16,256]{1,0:T(8,128)S(1)}, f32[16,256]{1,0:T(8,128)S(1)}, u32[]{:S(2)}, u32[]{:S(2)}) collective-permute-start(f32[16,256]{1,0:T(8,128)S(1)} %get-tuple-element.128), channel_id=1, source_target_pairs={{0,6},{1,7},{2,4},{3,5},{4,2},{5,3},{6,0},{7,1},{8,14},{9,15},{10,... | collective-permute-start | bytes 49160 | tf_op jit(solution)/shard_map/ppermute | solution.py:268
  34.3 4.5 %collective-permute-start.16 = (f32[16,256]{1,0:T(8,128)S(1)}, f32[16,256]{1,0:T(8,128)S(1)}, u32[]{:S(2)}, u32[]{:S(2)}) collective-permute-start(f32[16,256]{1,0:T(8,128)S(1)} %get-tuple-element.126), channel_id=1, source_target_pairs={{0,2},{1,3},{2,0},{3,1},{4,6},{5,7},{6,4},{7,5},{8,10},{9,11},{10,... | collective-permute-start | bytes 49160 | tf_op jit(solution)/shard_map/ppermute | solution.py:268
  38.9 0.6 %copy-start.2 = (f32[256]{0:T(256)}, f32[256]{0:T(256)S(1)}, u32[]{:S(2)}) copy-start(f32[256]{0:T(256)S(1)} %get-tuple-element.300) | copy-start | bytes 3076
where the time goes:
time: 39 us; the launch traced here: 39.5 us
  starting transfers between devices  22.3 us (57%)
  Pallas kernels  10.3 us (26%)
  waiting for transfers between devices  4.67 us (12%)
  local copies, waits for them, and re-layouts  1.24 us (3%)
  between operations  0.84 us (2%)
    ppermute x10, starting transfers between devices, swap(): return lax.ppermute(x, AXIS, [(i, i ^ bit) for i in range(n)])  10.8 us
    pallas_call x2, Pallas kernels, tiles(): pl.pallas_call(functools.partial(tile_kernel, counts, len(rights), tuple(...  7.3 us
    ppermute x1, starting transfers between devices, from_below(): return lax.ppermute(x, AXIS, [(i, i + PLANE) for i in range(n - PLANE)])  5.38 us
    all_to_all x1, starting transfers between devices, local(): lax.all_to_all(message, AXIS, split_axis=0, concat_axis=0, tiled=True)  4.89 us
    ppermute x10, waiting for transfers between devices, swap(): return lax.ppermute(x, AXIS, [(i, i ^ bit) for i in range(n)])  4.66 us
    ppermute x1, starting transfers between devices, from_above(): return lax.ppermute(x, AXIS, [(i + PLANE, i) for i in range(n - PLANE)])  1.28 us
    pallas_call x1, Pallas kernels, normalise(): pl.pallas_call(normalise_kernel, name='normalise', in_specs=[pl.BlockSpec...  1.26 us
    unnamed x10, local copies, waits for them, and re-layouts  1.24 us
  transfers between devices with their start and end apart: 13, of which 3 were waited for; matrix products, arithmetic and copies ran while one was open for 0% of the time, Pallas kernels for 23%

commit v1 on v0

--- a/solution.py
+++ b/solution.py
@@ -129,23 +129,19 @@
     return cap, span[0]
 
 
-def halves_kernel(x_ref, y_ref, first_ref, second_ref):
-    first_ref[...] = x_ref[: first_ref.shape[0]]
-    second_ref[...] = y_ref[first_ref.shape[0] :]
-
-
-def halves(x, y):
+def half_kernel(top, x_ref, half_ref):
+    half_ref[...] = x_ref[top : top + half_ref.shape[0]]
+
+
+def half_of(x, lower):
     half = (x.shape[0] - LABEL_ROWS) // 2
     return pl.pallas_call(
-        halves_kernel,
-        name="halves",
-        out_shape=[
-            jax.ShapeDtypeStruct((half, x.shape[1]), x.dtype),
-            jax.ShapeDtypeStruct((half + LABEL_ROWS, x.shape[1]), x.dtype),
-        ],
+        functools.partial(half_kernel, half if lower else 0),
+        name="lower_half" if lower else "upper_half",
+        out_shape=jax.ShapeDtypeStruct((half + LABEL_ROWS * lower, x.shape[1]), x.dtype),
         compiler_params=pltpu.CompilerParams(vmem_limit_bytes=4 * 1024 * 1024),
-        cost_estimate=pl.CostEstimate(flops=0, bytes_accessed=x.size * 4, transcendentals=0),
-    )(x, y)
+        cost_estimate=pl.CostEstimate(flops=0, bytes_accessed=x.size * 2, transcendentals=0),
+    )(x)
 
 
 def arrived_kernel(first_ref, second_ref, token_ref):
@@ -168,7 +164,7 @@
     parts, copies = [], []
     n_operands = sum(max(count, 1) for count in counts)
     tail = refs[n_operands + n_before + n_token :]
-    outs, scratch = tail[:n_right], tail[n_right:]
+    outs, down, scratch = tail[:n_right], tail[n_right], tail[n_right + 1 :]
     operands, before = list(refs[:n_operands]), refs[n_operands : n_operands + n_before]
     sem = 0
     for count in counts:
@@ -197,6 +193,10 @@
                 copy.wait()
             label = parts[k][rows:, :rows].astype(jnp.float32)[:1]
             labels[k] = label, jnp.min(label), jnp.max(label)
+            if k >= n_right:
+                for b in range(blocks):
+                    at = slice(b * BLOCK, (b + 1) * BLOCK)
+                    down[k - n_right, at] = jnp.broadcast_to(label[:, at], (BLOCK, BLOCK)).T
         return labels[k]
 
     def tile(r, c):
@@ -208,8 +208,7 @@
         )
         for b in range(blocks):
             at = slice(b * BLOCK, (b + 1) * BLOCK)
-            label = jnp.broadcast_to(labels[n_right + c][0][:, at], (BLOCK, BLOCK)).T
-            label = jnp.concatenate([label] * blocks, axis=1)
+            label = jnp.concatenate([down[c, at]] * blocks, axis=1)
             same = label == labels[r][0]
             part = sims[at]
             if own_first and c == 0 and r == 0:
@@ -219,15 +218,26 @@
             row = places[c] + b
             outs[r][row : row + 1, :] = jnp.max(part, axis=0, keepdims=True)
 
-    todo = [
-        (r, c)
-        for c in range(len(places))
-        for r in range(n_right)
-        if r >= n_before or places[c] >= before[r].shape[0]
-    ]
-    for r, c in sorted(todo, key=lambda rc: (len(copies[n_right + rc[1]]), len(copies[rc[0]]))):
-        right, left = labels_of(r), labels_of(n_right + c)
-        pl.when((left[1] <= right[2]) & (right[1] <= left[2]))(functools.partial(tile, r, c))
+    for chip in range(0, len(places), 2):
+        todo = [
+            (r, c)
+            for c in range(chip, min(chip + 2, len(places)))
+            for r in range(n_right)
+            if r >= n_before or places[c] >= before[r].shape[0]
+        ]
+        meet = False
+        for r, c in todo:
+            right, left = labels_of(r), labels_of(n_right + c)
+            meet |= (left[1] <= right[2]) & (right[1] <= left[2])
+
+        def chip_tiles(todo=todo):
+            for r, c in todo:
+                tile(r, c)
+
+        if own_first:
+            chip_tiles()
+        else:
+            pl.when(meet)(chip_tiles)
 
 
 def tiles(name, rights, lefts, places, own_first, before=(), token=None, flops=None):
@@ -242,8 +252,9 @@
     vmem, anywhere = pl.BlockSpec(memory_space=pltpu.VMEM), pl.BlockSpec(memory_space=pl.ANY)
     specs = [spec for count in counts for spec in ([anywhere] * count if count else [vmem])]
     extra = list(before) + ([] if token is None else [token])
-    scratch = [pltpu.VMEM((height_in, depth), jnp.bfloat16) for count in counts if count]
-    if scratch:
+    scratch = [pltpu.VMEM((len(lefts), rows, BLOCK), jnp.float32)]
+    scratch += [pltpu.VMEM((height_in, depth), jnp.bfloat16) for count in counts if count]
+    if sum(counts):
         scratch.append(pltpu.SemaphoreType.DMA((sum(counts),)))
     return pl.pallas_call(
         functools.partial(tile_kernel, counts, len(rights), tuple(places), rows, own_first, len(before), len(extra) - len(before)),
@@ -283,8 +294,8 @@
     above, below = from_above(unit), from_below(unit)
     twin = swap(unit, 1)
     message = message_of(requests, pair_left, pair_right, cluster_id)
-    along_x, message = lax.optimization_barrier((along_x, message))
-    first, second = halves(along_x, along_y)
+    along_y, _ = lax.optimization_barrier((along_y, message))
+    first, second = half_of(along_x, False), half_of(along_y, True)
     pieces = [swap(first, 4), swap(second, 2)]
     along_x, first = lax.optimization_barrier((along_x, first))
     above_twin, below_twin = swap(above, 1), swap(below, 1)

time: 39 us -> 39.2 us (level); the launches traced: 39.5 us -> 39 us
  Pallas kernels: 10.3 us -> 7.53 us
  waiting for transfers between devices: 4.67 us -> 6.19 us
  starting transfers between devices: 22.3 us -> 23.2 us
    pallas_call x2, Pallas kernels: 7.3 us -> 4.49 us  [tiles(): pl.pallas_call(functools.partial(tile_kernel, counts, len(rights), tuple(...]
    ppermute x10, waiting for transfers between devices: 4.66 us -> 6.18 us  [swap(): return lax.ppermute(x, AXIS, [(i, i ^ bit) for i in range(n)])]
    ppermute x10, starting transfers between devices: 10.8 us -> 12 us  [swap(): return lax.ppermute(x, AXIS, [(i, i ^ bit) for i in range(n)])]
    all_to_all x1, starting transfers between devices: 4.89 us -> 4.49 us  [local(): lax.all_to_all(message, AXIS, split_axis=0, concat_axis=0, tiled=True)]
  transfers between devices with their start and end apart: 13 -> 13, of which waited for: 3 -> 5; matrix products, arithmetic and copies ran while one was open for 0% -> 0% of each run, Pallas kernels for 23% -> 16%
where the time goes in v1:
time: 39.2 us; the launch traced here: 39 us
  starting transfers between devices  23.2 us (59%)
  Pallas kernels  7.53 us (19%)
  waiting for transfers between devices  6.19 us (16%)
  local copies, waits for them, and re-layouts  1.24 us (3%)
  between operations  0.81 us (2%)
    ppermute x10, starting transfers between devices, swap(): return lax.ppermute(x, AXIS, [(i, i ^ bit) for i in range(n)])  12 us
    ppermute x10, waiting for transfers between devices, swap(): return lax.ppermute(x, AXIS, [(i, i ^ bit) for i in range(n)])  6.18 us
    ppermute x1, starting transfers between devices, from_below(): return lax.ppermute(x, AXIS, [(i, i + PLANE) for i in range(n - PLANE)])  5.4 us
    all_to_all x1, starting transfers between devices, local(): lax.all_to_all(message, AXIS, split_axis=0, concat_axis=0, tiled=True)  4.49 us
    pallas_call x2, Pallas kernels, tiles(): pl.pallas_call(functools.partial(tile_kernel, counts, len(rights), tuple(...  4.49 us
    ppermute x1, starting transfers between devices, from_above(): return lax.ppermute(x, AXIS, [(i + PLANE, i) for i in range(n - PLANE)])  1.28 us
    pallas_call x1, Pallas kernels, normalise(): pl.pallas_call(normalise_kernel, name='normalise', in_specs=[pl.BlockSpec...  1.26 us
    unnamed x10, local copies, waits for them, and re-layouts  1.24 us
  transfers between devices with their start and end apart: 13, of which 5 were waited for; matrix products, arithmetic and copies ran while one was open for 0% of the time, Pallas kernels for 16%

profile of v1, /device:TPU:0, one launch (start us, length us, event | category | flops | bytes accessed | tf_op | source)
XLA Modules:
  0.0 39.0 jit_solution(10375076494140347918)
XLA Ops:
  0.0 1.3 %normalise.1.refs_0_.refs_3_.refs_5_ = bf16[272,1024]{1,0:T(8,128)(2,1)S(1)} custom-call(bf16[256,1024]{1,0:T(8,128)(2,1)} %x_hbm.1, s32[1,256]{1,0:T(1,128)} %bitcast.24), custom_call_target="tpu_custom_call" | custom-call | tf_op jit(solution)/shard_map/normalise/pallas_call | solution.py:39
  1.3 0.0 copy-start.4
  1.3 3.0 %collective-permute-start.8 = (bf16[272,1024]{1,0:T(8,128)(2,1)S(1)}, bf16[272,1024]{1,0:T(8,128)(2,1)S(1)}, u32[]{:S(2)}, u32[]{:S(2)}) collective-permute-start(bf16[272,1024]{1,0:T(8,128)(2,1)S(1)} %normalise.1.refs_0_.refs_3_.refs_5_), channel_id=1, source_target_pairs={{0,4},{1,5},{2,6},{3,7},{4,0},{5,1},{6,2},{7,3},{8,12},{9,13},{10,... | collective-permute-start | bytes 1671176 | tf_op jit(solution)/shard_map/ppermute | solution.py:279
  4.3 1.5 %collective-permute-start.7 = (bf16[272,1024]{1,0:T(8,128)(2,1)S(1)}, bf16[272,1024]{1,0:T(8,128)(2,1)S(1)}, u32[]{:S(2)}, u32[]{:S(2)}) collective-permute-start(bf16[272,1024]{1,0:T(8,128)(2,1)S(1)} %normalise.1.refs_0_.refs_3_.refs_5_), channel_id=1, source_target_pairs={{0,2},{1,3},{2,0},{3,1},{4,6},{5,7},{6,4},{7,5},{8,10},{9,11},{10,... | collective-permute-start | bytes 1671176 | tf_op jit(solution)/shard_map/ppermute | solution.py:279
  5.8 1.3 %collective-permute-start.12 = (bf16[272,1024]{1,0:T(8,128)(2,1)S(1)}, bf16[272,1024]{1,0:T(8,128)(2,1)S(1)}, u32[]{:S(2)}, u32[]{:S(2)}) collective-permute-start(bf16[272,1024]{1,0:T(8,128)(2,1)S(1)} %normalise.1.refs_0_.refs_3_.refs_5_), channel_id=1, source_target_pairs={{8,0},{9,1},{10,2},{11,3},{12,4},{13,5},{14,6},{15,7},{16,8},{17,9... | collective-permute-start | bytes 1671176 | tf_op jit(solution)/shard_map/ppermute | solution.py:282
  7.1 5.4 %collective-permute-start.14 = (bf16[272,1024]{1,0:T(8,128)(2,1)S(1)}, bf16[272,1024]{1,0:T(8,128)(2,1)}, u32[]{:S(2)}, u32[]{:S(2)}) collective-permute-start(bf16[272,1024]{1,0:T(8,128)(2,1)S(1)} %normalise.1.refs_0_.refs_3_.refs_5_), channel_id=1, source_target_pairs={{0,8},{1,9},{2,10},{3,11},{4,12},{5,13},{6,14},{7,15},{8,16},{9,17... | collective-permute-start | bytes 1671176 | tf_op jit(solution)/shard_map/ppermute | solution.py:285
  12.5 0.0 collective-permute-start.11
  12.5 0.0 copy-start
  12.5 0.0 copy-start.1
  12.5 0.7 %copy-done = s32[256]{0:T(256)S(1)} copy-done((s32[256]{0:T(256)S(1)}, s32[256]{0:T(256)}, u32[]{:S(2)}) %copy-start) | copy-done | bytes 1048
  13.2 0.8 %message.1 = f32[32,1,128]{2,1,0:T(1,128)} custom-call(s32[1,384]{1,0:T(1,128)S(1)} %reshape.16.left_ref, s32[1,384]{1,0:T(1,128)S(1)} %reshape.17.right_ref, s32[1,32]{1,0:T(1,128)S(1)} %bitcast.26, s32[1,256]{1,0:T(1,128)S(1)} %bitcast.25), custom_call_target="tpu_custom_call" | custom-call | tf_op jit(solution)/shard_map/message/pallas_call | solution.py:72
  14.1 2.9 %collective-permute-done.8.x_ref.refs_2_ = bf16[272,1024]{1,0:T(8,128)(2,1)S(1)} collective-permute-done((bf16[272,1024]{1,0:T(8,128)(2,1)S(1)}, bf16[272,1024]{1,0:T(8,128)(2,1)S(1)}, u32[]{:S(2)}, u32[]{:S(2)}) %collective-permute-start.8) | collective-permute-done | bytes 557088 | tf_op jit(solution)/shard_map/ppermute | solution.py:279
  17.0 1.8 %collective-permute-start.10 = (bf16[144,1024]{1,0:T(8,128)(2,1)S(1)}, bf16[144,1024]{1,0:T(8,128)(2,1)}, u32[]{:S(2)}, u32[]{:S(2)}) collective-permute-start(bf16[144,1024]{1,0:T(8,128)(2,1)S(1)} %lower_half.1), channel_id=1, source_target_pairs={{0,2},{1,3},{2,0},{3,1},{4,6},{5,7},{6,4},{7,5},{8,10},{9,11},{10,... | collective-permute-start | bytes 884744 | tf_op jit(solution)/shard_map/ppermute | solution.py:279
  18.8 1.6 %collective-permute-start.9 = (bf16[128,1024]{1,0:T(8,128)(2,1)S(1)}, bf16[128,1024]{1,0:T(8,128)(2,1)}, u32[]{:S(2)}, u32[]{:S(2)}) collective-permute-start(bf16[128,1024]{1,0:T(8,128)(2,1)S(1)} %upper_half.1), channel_id=1, source_target_pairs={{0,4},{1,5},{2,6},{3,7},{4,0},{5,1},{6,2},{7,3},{8,12},{9,13},{10,... | collective-permute-start | bytes 786440 | tf_op jit(solution)/shard_map/ppermute | solution.py:279
  20.4 4.5 %all-to-all-start = ((f32[32,1,128]{2,1,0:T(1,128)}), f32[32,1,128]{2,1,0:T(1,128)S(1)}, u32[]{:S(2)}, u32[]{:S(2)}) async-start(f32[32,1,128]{2,1,0:T(1,128)} %message.1), calls=%async_computation | async-start | bytes 32768 | tf_op jit(solution)/shard_map/all_to_all | solution.py:303
  24.9 0.3 collective-permute-start.13
  25.2 0.0 collective-permute-done.14.refs_9_
  25.2 0.3 collective-permute-start.15
  25.4 0.0 collective-permute-done.11.refs_4_.refs_6_
  25.4 1.0 %plane_tiles.1 = (f32[8,256]{1,0:T(8,128)S(1)}, f32[8,256]{1,0:T(8,128)S(1)}, f32[8,256]{1,0:T(8,128)S(1)}) custom-call(bf16[272,1024]{1,0:T(8,128)(2,1)S(1)} %normalise.1.refs_0_.refs_3_.refs_5_, bf16[272,1024]{1,0:T(8,128)(2,1)S(1)} %collective-permute-done.7.x_ref.refs_1_, bf16[272,1024]{1,0:T(8,128)(2,1)S(1)} %collective-permute-done.8.x_ref.refs_2_, ...), custom_call_target="tpu_custom_call" | custom-call | flops 805306368 | bytes 2621440 | tf_op jit(solution)/shard_map/plane_tiles/pallas_call | solution.py:259
  26.5 0.0 collective-permute-done.9.first_ref.refs_3_
  26.5 0.4 collective-permute-done.13.refs_8_
  26.9 1.0 %collective-permute-done.15.refs_10_ = bf16[272,1024]{1,0:T(8,128)(2,1)S(1)} collective-permute-done((bf16[272,1024]{1,0:T(8,128)(2,1)}, bf16[272,1024]{1,0:T(8,128)(2,1)S(1)}, u32[]{:S(2)}, u32[]{:S(2)}) %collective-permute-start.15) | collective-permute-done | bytes 557088 | tf_op jit(solution)/shard_map/ppermute | solution.py:279
  27.9 3.4 %all_tiles.1 = (f32[16,256]{1,0:T(8,128)S(1)}, f32[16,256]{1,0:T(8,128)S(1)}, f32[16,256]{1,0:T(8,128)S(1)}, f32[16,256]{1,0:T(8,128)S(1)}) custom-call(bf16[272,1024]{1,0:T(8,128)(2,1)S(1)} %normalise.1.refs_0_.refs_3_.refs_5_, bf16[272,1024]{1,0:T(8,128)(2,1)S(1)} %collective-permute-done.7.x_ref.refs_1_, ...), custom_call_target="tpu_custom_call" | custom-call | bytes 5767168 | tf_op jit(solution)/shard_map/all_tiles/pallas_call | solution.py:259
  31.3 0.6 %collective-permute-start.17 = (f32[16,256]{1,0:T(8,128)S(1)}, f32[16,256]{1,0:T(8,128)S(1)}, u32[]{:S(2)}, u32[]{:S(2)}) collective-permute-start(f32[16,256]{1,0:T(8,128)S(1)} %get-tuple-element.121), channel_id=1, source_target_pairs={{0,4},{1,5},{2,6},{3,7},{4,0},{5,1},{6,2},{7,3},{8,12},{9,13},{10,... | collective-permute-start | bytes 49160 | tf_op jit(solution)/shard_map/ppermute | solution.py:279
  31.9 2.7 %collective-permute-start.18 = (f32[16,256]{1,0:T(8,128)S(1)}, f32[16,256]{1,0:T(8,128)S(1)}, u32[]{:S(2)}, u32[]{:S(2)}) collective-permute-start(f32[16,256]{1,0:T(8,128)S(1)} %get-tuple-element.122), channel_id=1, source_target_pairs={{0,6},{1,7},{2,4},{3,5},{4,2},{5,3},{6,0},{7,1},{8,14},{9,15},{10,... | collective-permute-start | bytes 49160 | tf_op jit(solution)/shard_map/ppermute | solution.py:279
  34.6 0.3 collective-permute-start.16
  34.9 0.9 %cover.2 = (f32[4,16,256]{2,1,0:T(8,128)S(1)}, s32[1]{0:T(128)}) custom-call(s32[1]{0:T(128)} %constant.4.clone.1.offset_ref, f32[32,1,128]{2,1,0:T(1,128)S(1)} %all-to-all-done.heard_ref), custom_call_target="tpu_custom_call" | custom-call | tf_op jit(solution)/shard_map/cover/pallas_call | solution.py:118
  36.5 0.1 collective-permute-done.18
  36.5 1.8 %collective-permute-done.16 = f32[16,256]{1,0:T(8,128)S(1)} collective-permute-done((f32[16,256]{1,0:T(8,128)S(1)}, f32[16,256]{1,0:T(8,128)S(1)}, u32[]{:S(2)}, u32[]{:S(2)}) %collective-permute-start.16) | collective-permute-done | bytes 16416 | tf_op jit(solution)/shard_map/ppermute | solution.py:279
  38.4 0.0 copy-start.2
  38.5 0.6 %copy-done.2 = f32[256]{0:T(256)} copy-done((f32[256]{0:T(256)}, f32[256]{0:T(256)S(1)}, u32[]{:S(2)}) %copy-start.2) | copy-done | bytes 1048
  (17 shorter events, 0.1 us)
Async XLA Ops:
  0.0 12.5 %copy-start.3 = (s32[384]{0:T(512)S(1)}, s32[384]{0:T(512)}, u32[]{:S(2)}) copy-start(s32[384]{0:T(512)} %param.12) | copy-start | bytes 4612
  1.3 11.2 %copy-start.4 = (s32[384]{0:T(512)S(1)}, s32[384]{0:T(512)}, u32[]{:S(2)}) copy-start(s32[384]{0:T(512)} %param.13) | copy-start | bytes 4612
  1.3 15.7 %collective-permute-start.8 = (bf16[272,1024]{1,0:T(8,128)(2,1)S(1)}, bf16[272,1024]{1,0:T(8,128)(2,1)S(1)}, u32[]{:S(2)}, u32[]{:S(2)}) collective-permute-start(bf16[272,1024]{1,0:T(8,128)(2,1)S(1)} %normalise.1.refs_0_.refs_3_.refs_5_), channel_id=1, source_target_pairs={{0,4},{1,5},{2,6},{3,7},{4,0},{5,1},{6,2},{7,3},{8,12},{9,13},{10,... | collective-permute-start | bytes 1671176 | tf_op jit(solution)/shard_map/ppermute | solution.py:279
  4.3 14.4 %collective-permute-start.7 = (bf16[272,1024]{1,0:T(8,128)(2,1)S(1)}, bf16[272,1024]{1,0:T(8,128)(2,1)S(1)}, u32[]{:S(2)}, u32[]{:S(2)}) collective-permute-start(bf16[272,1024]{1,0:T(8,128)(2,1)S(1)} %normalise.1.refs_0_.refs_3_.refs_5_), channel_id=1, source_target_pairs={{0,2},{1,3},{2,0},{3,1},{4,6},{5,7},{6,4},{7,5},{8,10},{9,11},{10,... | collective-permute-start | bytes 1671176 | tf_op jit(solution)/shard_map/ppermute | solution.py:279
  5.8 19.0 %collective-permute-start.12 = (bf16[272,1024]{1,0:T(8,128)(2,1)S(1)}, bf16[272,1024]{1,0:T(8,128)(2,1)S(1)}, u32[]{:S(2)}, u32[]{:S(2)}) collective-permute-start(bf16[272,1024]{1,0:T(8,128)(2,1)S(1)} %normalise.1.refs_0_.refs_3_.refs_5_), channel_id=1, source_target_pairs={{8,0},{9,1},{10,2},{11,3},{12,4},{13,5},{14,6},{15,7},{16,8},{17,9... | collective-permute-start | bytes 1671176 | tf_op jit(solution)/shard_map/ppermute | solution.py:282
  7.1 18.1 %collective-permute-start.14 = (bf16[272,1024]{1,0:T(8,128)(2,1)S(1)}, bf16[272,1024]{1,0:T(8,128)(2,1)}, u32[]{:S(2)}, u32[]{:S(2)}) collective-permute-start(bf16[272,1024]{1,0:T(8,128)(2,1)S(1)} %normalise.1.refs_0_.refs_3_.refs_5_), channel_id=1, source_target_pairs={{0,8},{1,9},{2,10},{3,11},{4,12},{5,13},{6,14},{7,15},{8,16},{9,17... | collective-permute-start | bytes 1671176 | tf_op jit(solution)/shard_map/ppermute | solution.py:285
  12.5 12.9 %collective-permute-start.11 = (bf16[272,1024]{1,0:T(8,128)(2,1)S(1)}, bf16[272,1024]{1,0:T(8,128)(2,1)S(1)}, u32[]{:S(2)}, u32[]{:S(2)}) collective-permute-start(bf16[272,1024]{1,0:T(8,128)(2,1)S(1)} %normalise.1.refs_0_.refs_3_.refs_5_), channel_id=1, source_target_pairs={{0,1},{1,0},{2,3},{3,2},{4,5},{5,4},{6,7},{7,6},{8,9},{9,8},{10,11... | collective-permute-start | bytes 1671176 | tf_op jit(solution)/shard_map/ppermute | solution.py:279
  12.5 0.7 %copy-start = (s32[256]{0:T(256)S(1)}, s32[256]{0:T(256)}, u32[]{:S(2)}) copy-start(s32[256]{0:T(256)} %param.10) | copy-start | bytes 3076
  12.5 0.7 %copy-start.1 = (s32[32]{0:T(128)S(1)}, s32[32]{0:T(128)}, u32[]{:S(2)}) copy-start(s32[32]{0:T(128)} %param.11) | copy-start | bytes 388
  17.0 9.5 %collective-permute-start.10 = (bf16[144,1024]{1,0:T(8,128)(2,1)S(1)}, bf16[144,1024]{1,0:T(8,128)(2,1)}, u32[]{:S(2)}, u32[]{:S(2)}) collective-permute-start(bf16[144,1024]{1,0:T(8,128)(2,1)S(1)} %lower_half.1), channel_id=1, source_target_pairs={{0,2},{1,3},{2,0},{3,1},{4,6},{5,7},{6,4},{7,5},{8,10},{9,11},{10,... | collective-permute-start | bytes 884744 | tf_op jit(solution)/shard_map/ppermute | solution.py:279
  18.8 7.7 %collective-permute-start.9 = (bf16[128,1024]{1,0:T(8,128)(2,1)S(1)}, bf16[128,1024]{1,0:T(8,128)(2,1)}, u32[]{:S(2)}, u32[]{:S(2)}) collective-permute-start(bf16[128,1024]{1,0:T(8,128)(2,1)S(1)} %upper_half.1), channel_id=1, source_target_pairs={{0,4},{1,5},{2,6},{3,7},{4,0},{5,1},{6,2},{7,3},{8,12},{9,13},{10,... | collective-permute-start | bytes 786440 | tf_op jit(solution)/shard_map/ppermute | solution.py:279
  20.4 14.6 %all-to-all-start = ((f32[32,1,128]{2,1,0:T(1,128)}), f32[32,1,128]{2,1,0:T(1,128)S(1)}, u32[]{:S(2)}, u32[]{:S(2)}) async-start(f32[32,1,128]{2,1,0:T(1,128)} %message.1), calls=%async_computation | async-start | bytes 32768 | tf_op jit(solution)/shard_map/all_to_all | solution.py:303
  24.9 2.0 %collective-permute-start.13 = (bf16[272,1024]{1,0:T(8,128)(2,1)S(1)}, bf16[272,1024]{1,0:T(8,128)(2,1)S(1)}, u32[]{:S(2)}, u32[]{:S(2)}) collective-permute-start(bf16[272,1024]{1,0:T(8,128)(2,1)S(1)} %collective-permute-done.12.refs_7_), channel_id=1, source_target_pairs={{0,1},{1,0},{2,3},{3,2},{4,5},{5,4},{6,7},{7,6},{8,9},{9,8},{10,11... | collective-permute-start | bytes 1671176 | tf_op jit(solution)/shard_map/ppermute | solution.py:279
  25.2 2.7 %collective-permute-start.15 = (bf16[272,1024]{1,0:T(8,128)(2,1)}, bf16[272,1024]{1,0:T(8,128)(2,1)S(1)}, u32[]{:S(2)}, u32[]{:S(2)}) collective-permute-start(bf16[272,1024]{1,0:T(8,128)(2,1)} %collective-permute-done.14.refs_9_), channel_id=1, source_target_pairs={{0,1},{1,0},{2,3},{3,2},{4,5},{5,4},{6,7},{7,6},{8,9},{9,8},{10,11... | collective-permute-start | bytes 1671176 | tf_op jit(solution)/shard_map/ppermute | solution.py:279
  31.3 5.1 %collective-permute-start.17 = (f32[16,256]{1,0:T(8,128)S(1)}, f32[16,256]{1,0:T(8,128)S(1)}, u32[]{:S(2)}, u32[]{:S(2)}) collective-permute-start(f32[16,256]{1,0:T(8,128)S(1)} %get-tuple-element.121), channel_id=1, source_target_pairs={{0,4},{1,5},{2,6},{3,7},{4,0},{5,1},{6,2},{7,3},{8,12},{9,13},{10,... | collective-permute-start | bytes 49160 | tf_op jit(solution)/shard_map/ppermute | solution.py:279
  31.9 4.6 %collective-permute-start.18 = (f32[16,256]{1,0:T(8,128)S(1)}, f32[16,256]{1,0:T(8,128)S(1)}, u32[]{:S(2)}, u32[]{:S(2)}) collective-permute-start(f32[16,256]{1,0:T(8,128)S(1)} %get-tuple-element.122), channel_id=1, source_target_pairs={{0,6},{1,7},{2,4},{3,5},{4,2},{5,3},{6,0},{7,1},{8,14},{9,15},{10,... | collective-permute-start | bytes 49160 | tf_op jit(solution)/shard_map/ppermute | solution.py:279
  34.6 3.7 %collective-permute-start.16 = (f32[16,256]{1,0:T(8,128)S(1)}, f32[16,256]{1,0:T(8,128)S(1)}, u32[]{:S(2)}, u32[]{:S(2)}) collective-permute-start(f32[16,256]{1,0:T(8,128)S(1)} %get-tuple-element.120), channel_id=1, source_target_pairs={{0,2},{1,3},{2,0},{3,1},{4,6},{5,7},{6,4},{7,5},{8,10},{9,11},{10,... | collective-permute-start | bytes 49160 | tf_op jit(solution)/shard_map/ppermute | solution.py:279
  38.4 0.6 %copy-start.2 = (f32[256]{0:T(256)}, f32[256]{0:T(256)S(1)}, u32[]{:S(2)}) copy-start(f32[256]{0:T(256)S(1)} %get-tuple-element.294) | copy-start | bytes 3076

commit v2 on v1

--- a/solution.py
+++ b/solution.py
@@ -160,11 +160,20 @@
     )(*pieces)
 
 
-def tile_kernel(counts, n_right, places, rows, own_first, n_before, n_token, *refs):
+def tile_kernel(counts, n_right, places, rows, own_first, n_before, n_token, keep, *refs):
     parts, copies = [], []
     n_operands = sum(max(count, 1) for count in counts)
     tail = refs[n_operands + n_before + n_token :]
-    outs, down, scratch = tail[:n_right], tail[n_right], tail[n_right + 1 :]
+    outs, kept, tail = tail[:n_right], tail[n_right : n_right + len(keep)], tail[n_right + len(keep) :]
+    down, scratch = tail[0], tail[1:]
+    keeping = {}
+
+    def put_away(k):
+        if k in keep:
+            at = keep.index(k)
+            keeping[k] = pltpu.make_async_copy(parts[k], kept[at], scratch[-1].at[sum(counts) + at])
+            keeping[k].start()
+
     operands, before = list(refs[:n_operands]), refs[n_operands : n_operands + n_before]
     sem = 0
     for count in counts:
@@ -172,6 +181,7 @@
         if not count:
             parts.append(here[0])
             copies.append([])
+            put_away(len(parts) - 1)
             continue
         part, top, own = scratch[sum(1 for c in copies if c)], 0, []
         for piece in here:
@@ -191,8 +201,10 @@
         if k not in labels:
             for copy in copies[k]:
                 copy.wait()
+            if copies[k]:
+                put_away(k)
             label = parts[k][rows:, :rows].astype(jnp.float32)[:1]
-            labels[k] = label, jnp.min(label), jnp.max(label)
+            labels[k] = label, label[0, 0], label[0, rows - 1]
             if k >= n_right:
                 for b in range(blocks):
                     at = slice(b * BLOCK, (b + 1) * BLOCK)
@@ -238,9 +250,11 @@
             chip_tiles()
         else:
             pl.when(meet)(chip_tiles)
-
-
-def tiles(name, rights, lefts, places, own_first, before=(), token=None, flops=None):
+    for copy in keeping.values():
+        copy.wait()
+
+
+def tiles(name, rights, lefts, places, own_first, before=(), token=None, flops=None, keep=()):
     parts = list(rights) + list(lefts)
     counts = tuple(len(part) if isinstance(part, list) else 0 for part in parts)
     operands = [piece for part in parts for piece in (part if isinstance(part, list) else [part])]
@@ -254,14 +268,15 @@
     extra = list(before) + ([] if token is None else [token])
     scratch = [pltpu.VMEM((len(lefts), rows, BLOCK), jnp.float32)]
     scratch += [pltpu.VMEM((height_in, depth), jnp.bfloat16) for count in counts if count]
-    if sum(counts):
-        scratch.append(pltpu.SemaphoreType.DMA((sum(counts),)))
-    return pl.pallas_call(
-        functools.partial(tile_kernel, counts, len(rights), tuple(places), rows, own_first, len(before), len(extra) - len(before)),
+    if sum(counts) + len(keep):
+        scratch.append(pltpu.SemaphoreType.DMA((sum(counts) + len(keep),)))
+    return pl.pallas_call(
+        functools.partial(tile_kernel, counts, len(rights), tuple(places), rows, own_first, len(before), len(extra) - len(before), keep),
         name=name,
         in_specs=specs + [vmem] * len(extra),
-        out_specs=[vmem] * len(rights),
-        out_shape=[jax.ShapeDtypeStruct((height, rows), jnp.float32)] * len(rights),
+        out_specs=[vmem] * len(rights) + [pl.BlockSpec(memory_space=pltpu.HBM)] * len(keep),
+        out_shape=[jax.ShapeDtypeStruct((height, rows), jnp.float32)] * len(rights)
+        + [jax.ShapeDtypeStruct((height_in, depth), jnp.bfloat16)] * len(keep),
         scratch_shapes=scratch,
         compiler_params=pltpu.CompilerParams(vmem_limit_bytes=VMEM_TILES),
         cost_estimate=pl.CostEstimate(
@@ -308,7 +323,7 @@
     near_rights = [unit, along_x, along_y]
     plane_parts = tiles("plane_tiles", near_rights, [unit, twin], plane_places, True)
     token = arrived(pieces)
-    parts = tiles(
+    *parts, across = tiles(
         "all_tiles",
         near_rights + [pieces],
         [unit, twin] + lefts,
@@ -317,6 +332,7 @@
         plane_parts,
         token,
         flops=0,
+        keep=(3,),
     )
     cap, span = cover(heard, 1, blk_dev, rows)
     best = owners_best(parts, cap)
@@ -328,7 +344,7 @@
             lefts = [above, swap(above, 1), below, swap(below, 1)]
             parts = tiles(
                 "further_tiles",
-                near_rights + [pieces],
+                near_rights + [across],
                 lefts,
                 [blk_dev * k for k in range(4)],
                 False,

time: 39.2 us -> 38.6 us (0.985)
  Pallas kernels: 7.53 us -> 6.88 us
    pallas_call x2, Pallas kernels: 4.49 us -> 3.84 us  [tiles(): pl.pallas_call(functools.partial(tile_kernel, counts, len(rights), tuple(...]
  transfers between devices with their start and end apart: 13 -> 13, of which waited for: 5 -> 5; matrix products, arithmetic and copies ran while one was open for 0% -> 0% of each run, Pallas kernels for 16% -> 15%
where the time goes in v2:
time: 38.6 us; the launch traced here: 38.4 us
  starting transfers between devices  23.2 us (60%)
  Pallas kernels  6.88 us (18%)
  waiting for transfers between devices  6.21 us (16%)
  local copies, waits for them, and re-layouts  1.24 us (3%)
  between operations  0.81 us (2%)
    ppermute x10, starting transfers between devices, swap(): return lax.ppermute(x, AXIS, [(i, i ^ bit) for i in range(n)])  12 us
    ppermute x10, waiting for transfers between devices, swap(): return lax.ppermute(x, AXIS, [(i, i ^ bit) for i in range(n)])  6.21 us
    ppermute x1, starting transfers between devices, from_below(): return lax.ppermute(x, AXIS, [(i, i + PLANE) for i in range(n - PLANE)])  5.38 us
    all_to_all x1, starting transfers between devices, local(): lax.all_to_all(message, AXIS, split_axis=0, concat_axis=0, tiled=True)  4.49 us
    pallas_call x2, Pallas kernels, tiles(): pl.pallas_call(functools.partial(tile_kernel, counts, len(rights), tuple(...  3.84 us
    ppermute x1, starting transfers between devices, from_above(): return lax.ppermute(x, AXIS, [(i + PLANE, i) for i in range(n - PLANE)])  1.28 us
    pallas_call x1, Pallas kernels, normalise(): pl.pallas_call(normalise_kernel, name='normalise', in_specs=[pl.BlockSpec...  1.26 us
    unnamed x10, local copies, waits for them, and re-layouts  1.24 us
  transfers between devices with their start and end apart: 13, of which 5 were waited for; matrix products, arithmetic and copies ran while one was open for 0% of the time, Pallas kernels for 15%

profile of v2, /device:TPU:0, one launch (start us, length us, event | category | flops | bytes accessed | tf_op | source)
XLA Modules:
  0.0 38.4 jit_solution(7834132308264091763)
XLA Ops:
  0.0 1.3 %normalise.1.refs_0_.refs_3_.refs_5_ = bf16[272,1024]{1,0:T(8,128)(2,1)S(1)} custom-call(bf16[256,1024]{1,0:T(8,128)(2,1)} %x_hbm.1, s32[1,256]{1,0:T(1,128)} %bitcast.24), custom_call_target="tpu_custom_call" | custom-call | tf_op jit(solution)/shard_map/normalise/pallas_call | solution.py:39
  1.3 0.0 copy-start.4
  1.3 3.0 %collective-permute-start.8 = (bf16[272,1024]{1,0:T(8,128)(2,1)S(1)}, bf16[272,1024]{1,0:T(8,128)(2,1)S(1)}, u32[]{:S(2)}, u32[]{:S(2)}) collective-permute-start(bf16[272,1024]{1,0:T(8,128)(2,1)S(1)} %normalise.1.refs_0_.refs_3_.refs_5_), channel_id=1, source_target_pairs={{0,4},{1,5},{2,6},{3,7},{4,0},{5,1},{6,2},{7,3},{8,12},{9,13},{10,... | collective-permute-start | bytes 1671176 | tf_op jit(solution)/shard_map/ppermute | solution.py:294
  4.3 1.5 %collective-permute-start.7 = (bf16[272,1024]{1,0:T(8,128)(2,1)S(1)}, bf16[272,1024]{1,0:T(8,128)(2,1)S(1)}, u32[]{:S(2)}, u32[]{:S(2)}) collective-permute-start(bf16[272,1024]{1,0:T(8,128)(2,1)S(1)} %normalise.1.refs_0_.refs_3_.refs_5_), channel_id=1, source_target_pairs={{0,2},{1,3},{2,0},{3,1},{4,6},{5,7},{6,4},{7,5},{8,10},{9,11},{10,... | collective-permute-start | bytes 1671176 | tf_op jit(solution)/shard_map/ppermute | solution.py:294
  5.8 1.3 %collective-permute-start.12 = (bf16[272,1024]{1,0:T(8,128)(2,1)S(1)}, bf16[272,1024]{1,0:T(8,128)(2,1)}, u32[]{:S(2)}, u32[]{:S(2)}) collective-permute-start(bf16[272,1024]{1,0:T(8,128)(2,1)S(1)} %normalise.1.refs_0_.refs_3_.refs_5_), channel_id=1, source_target_pairs={{8,0},{9,1},{10,2},{11,3},{12,4},{13,5},{14,6},{15,7},{16,8},{17,9... | collective-permute-start | bytes 1671176 | tf_op jit(solution)/shard_map/ppermute | solution.py:297
  7.1 5.4 %collective-permute-start.14 = (bf16[272,1024]{1,0:T(8,128)(2,1)S(1)}, bf16[272,1024]{1,0:T(8,128)(2,1)}, u32[]{:S(2)}, u32[]{:S(2)}) collective-permute-start(bf16[272,1024]{1,0:T(8,128)(2,1)S(1)} %normalise.1.refs_0_.refs_3_.refs_5_), channel_id=1, source_target_pairs={{0,8},{1,9},{2,10},{3,11},{4,12},{5,13},{6,14},{7,15},{8,16},{9,17... | collective-permute-start | bytes 1671176 | tf_op jit(solution)/shard_map/ppermute | solution.py:300
  12.5 0.0 collective-permute-start.11
  12.5 0.0 copy-start
  12.5 0.0 copy-start.1
  12.5 0.7 %copy-done = s32[256]{0:T(256)S(1)} copy-done((s32[256]{0:T(256)S(1)}, s32[256]{0:T(256)}, u32[]{:S(2)}) %copy-start) | copy-done | bytes 1048
  13.2 0.8 %message.1 = f32[32,1,128]{2,1,0:T(1,128)} custom-call(s32[1,384]{1,0:T(1,128)S(1)} %reshape.16.left_ref, s32[1,384]{1,0:T(1,128)S(1)} %reshape.17.right_ref, s32[1,32]{1,0:T(1,128)S(1)} %bitcast.26, s32[1,256]{1,0:T(1,128)S(1)} %bitcast.25), custom_call_target="tpu_custom_call" | custom-call | tf_op jit(solution)/shard_map/message/pallas_call | solution.py:72
  14.0 2.9 %collective-permute-done.8.x_ref.refs_2_ = bf16[272,1024]{1,0:T(8,128)(2,1)S(1)} collective-permute-done((bf16[272,1024]{1,0:T(8,128)(2,1)S(1)}, bf16[272,1024]{1,0:T(8,128)(2,1)S(1)}, u32[]{:S(2)}, u32[]{:S(2)}) %collective-permute-start.8) | collective-permute-done | bytes 557088 | tf_op jit(solution)/shard_map/ppermute | solution.py:294
  17.0 1.8 %collective-permute-start.10 = (bf16[144,1024]{1,0:T(8,128)(2,1)S(1)}, bf16[144,1024]{1,0:T(8,128)(2,1)S(1)}, u32[]{:S(2)}, u32[]{:S(2)}) collective-permute-start(bf16[144,1024]{1,0:T(8,128)(2,1)S(1)} %lower_half.1), channel_id=1, source_target_pairs={{0,2},{1,3},{2,0},{3,1},{4,6},{5,7},{6,4},{7,5},{8,10},{9,11},{10,... | collective-permute-start | bytes 884744 | tf_op jit(solution)/shard_map/ppermute | solution.py:294
  18.8 1.6 %collective-permute-start.9 = (bf16[128,1024]{1,0:T(8,128)(2,1)S(1)}, bf16[128,1024]{1,0:T(8,128)(2,1)S(1)}, u32[]{:S(2)}, u32[]{:S(2)}) collective-permute-start(bf16[128,1024]{1,0:T(8,128)(2,1)S(1)} %upper_half.1), channel_id=1, source_target_pairs={{0,4},{1,5},{2,6},{3,7},{4,0},{5,1},{6,2},{7,3},{8,12},{9,13},{10,... | collective-permute-start | bytes 786440 | tf_op jit(solution)/shard_map/ppermute | solution.py:294
  20.4 4.5 %all-to-all-start = ((f32[32,1,128]{2,1,0:T(1,128)}), f32[32,1,128]{2,1,0:T(1,128)S(1)}, u32[]{:S(2)}, u32[]{:S(2)}) async-start(f32[32,1,128]{2,1,0:T(1,128)} %message.1), calls=%async_computation | async-start | bytes 32768 | tf_op jit(solution)/shard_map/all_to_all | solution.py:318
  24.9 0.0 collective-permute-done.12.refs_7_
  24.9 0.3 collective-permute-start.13
  25.2 0.3 collective-permute-start.15
  25.4 0.0 collective-permute-done.11.refs_4_.refs_6_
  25.4 1.0 %plane_tiles.1 = (f32[8,256]{1,0:T(8,128)S(1)}, f32[8,256]{1,0:T(8,128)S(1)}, f32[8,256]{1,0:T(8,128)S(1)}) custom-call(bf16[272,1024]{1,0:T(8,128)(2,1)S(1)} %normalise.1.refs_0_.refs_3_.refs_5_, bf16[272,1024]{1,0:T(8,128)(2,1)S(1)} %collective-permute-done.7.x_ref.refs_1_, bf16[272,1024]{1,0:T(8,128)(2,1)S(1)} %collective-permute-done.8.x_ref.refs_2_, ...), custom_call_target="tpu_custom_call" | custom-call | flops 805306368 | bytes 2621440 | tf_op jit(solution)/shard_map/plane_tiles/pallas_call | solution.py:273
  26.5 0.0 collective-permute-done.9.first_ref.refs_3_
  26.5 0.6 %collective-permute-done.13.refs_8_ = bf16[272,1024]{1,0:T(8,128)(2,1)S(1)} collective-permute-done((bf16[272,1024]{1,0:T(8,128)(2,1)}, bf16[272,1024]{1,0:T(8,128)(2,1)S(1)}, u32[]{:S(2)}, u32[]{:S(2)}) %collective-permute-start.13) | collective-permute-done | bytes 557088 | tf_op jit(solution)/shard_map/ppermute | solution.py:294
  27.1 0.8 %collective-permute-done.15.refs_10_ = bf16[272,1024]{1,0:T(8,128)(2,1)S(1)} collective-permute-done((bf16[272,1024]{1,0:T(8,128)(2,1)}, bf16[272,1024]{1,0:T(8,128)(2,1)S(1)}, u32[]{:S(2)}, u32[]{:S(2)}) %collective-permute-start.15) | collective-permute-done | bytes 557088 | tf_op jit(solution)/shard_map/ppermute | solution.py:294
  27.9 2.8 %all_tiles.1 = (f32[16,256]{1,0:T(8,128)S(1)}, f32[16,256]{1,0:T(8,128)S(1)}, f32[16,256]{1,0:T(8,128)S(1)}, f32[16,256]{1,0:T(8,128)S(1)}, bf16[272,1024]{1,0:T(8,128)(2,1)S(1)}) custom-call(bf16[272,1024]{1,0:T(8,128)(2,1)S(1)} %normalise.1.refs_0_.refs_3_.refs_5_, bf16[272,1024]{1,0:T(8,128)(2,1)S(1)} %collective-permute-done.7.x_ref.refs_1_, ...), custom_call_target="tpu_custom_call" | custom-call | bytes 5767168 | tf_op jit(solution)/shard_map/all_tiles/pallas_call | solution.py:273
  30.7 1.8 %collective-permute-start.17 = (f32[16,256]{1,0:T(8,128)S(1)}, f32[16,256]{1,0:T(8,128)S(1)}, u32[]{:S(2)}, u32[]{:S(2)}) collective-permute-start(f32[16,256]{1,0:T(8,128)S(1)} %get-tuple-element.114), channel_id=1, source_target_pairs={{0,4},{1,5},{2,6},{3,7},{4,0},{5,1},{6,2},{7,3},{8,12},{9,13},{10,... | collective-permute-start | bytes 49160 | tf_op jit(solution)/shard_map/ppermute | solution.py:294
  32.5 1.5 %collective-permute-start.18 = (f32[16,256]{1,0:T(8,128)S(1)}, f32[16,256]{1,0:T(8,128)S(1)}, u32[]{:S(2)}, u32[]{:S(2)}) collective-permute-start(f32[16,256]{1,0:T(8,128)S(1)} %get-tuple-element.115), channel_id=1, source_target_pairs={{0,6},{1,7},{2,4},{3,5},{4,2},{5,3},{6,0},{7,1},{8,14},{9,15},{10,... | collective-permute-start | bytes 49160 | tf_op jit(solution)/shard_map/ppermute | solution.py:294
  34.0 0.3 collective-permute-start.16
  34.3 0.9 %cover.2 = (f32[4,16,256]{2,1,0:T(8,128)S(1)}, s32[1]{0:T(128)}) custom-call(s32[1]{0:T(128)} %constant.4.clone.1.offset_ref, f32[32,1,128]{2,1,0:T(1,128)S(1)} %all-to-all-done.heard_ref), custom_call_target="tpu_custom_call" | custom-call | tf_op jit(solution)/shard_map/cover/pallas_call | solution.py:118
  35.8 1.4 %collective-permute-done.18 = f32[16,256]{1,0:T(8,128)S(1)} collective-permute-done((f32[16,256]{1,0:T(8,128)S(1)}, f32[16,256]{1,0:T(8,128)S(1)}, u32[]{:S(2)}, u32[]{:S(2)}) %collective-permute-start.18) | collective-permute-done | bytes 16416 | tf_op jit(solution)/shard_map/ppermute | solution.py:294
  37.3 0.5 %collective-permute-done.16 = f32[16,256]{1,0:T(8,128)S(1)} collective-permute-done((f32[16,256]{1,0:T(8,128)S(1)}, f32[16,256]{1,0:T(8,128)S(1)}, u32[]{:S(2)}, u32[]{:S(2)}) %collective-permute-start.16) | collective-permute-done | bytes 16416 | tf_op jit(solution)/shard_map/ppermute | solution.py:294
  37.8 0.0 copy-start.2
  37.8 0.6 %copy-done.2 = f32[256]{0:T(256)} copy-done((f32[256]{0:T(256)}, f32[256]{0:T(256)S(1)}, u32[]{:S(2)}) %copy-start.2) | copy-done | bytes 1048
  (17 shorter events, 0.1 us)
Async XLA Ops:
  0.0 12.5 %copy-start.3 = (s32[384]{0:T(512)S(1)}, s32[384]{0:T(512)}, u32[]{:S(2)}) copy-start(s32[384]{0:T(512)} %param.12) | copy-start | bytes 4612
  1.3 11.2 %copy-start.4 = (s32[384]{0:T(512)S(1)}, s32[384]{0:T(512)}, u32[]{:S(2)}) copy-start(s32[384]{0:T(512)} %param.13) | copy-start | bytes 4612
  1.3 15.7 %collective-permute-start.8 = (bf16[272,1024]{1,0:T(8,128)(2,1)S(1)}, bf16[272,1024]{1,0:T(8,128)(2,1)S(1)}, u32[]{:S(2)}, u32[]{:S(2)}) collective-permute-start(bf16[272,1024]{1,0:T(8,128)(2,1)S(1)} %normalise.1.refs_0_.refs_3_.refs_5_), channel_id=1, source_target_pairs={{0,4},{1,5},{2,6},{3,7},{4,0},{5,1},{6,2},{7,3},{8,12},{9,13},{10,... | collective-permute-start | bytes 1671176 | tf_op jit(solution)/shard_map/ppermute | solution.py:294
  4.3 14.4 %collective-permute-start.7 = (bf16[272,1024]{1,0:T(8,128)(2,1)S(1)}, bf16[272,1024]{1,0:T(8,128)(2,1)S(1)}, u32[]{:S(2)}, u32[]{:S(2)}) collective-permute-start(bf16[272,1024]{1,0:T(8,128)(2,1)S(1)} %normalise.1.refs_0_.refs_3_.refs_5_), channel_id=1, source_target_pairs={{0,2},{1,3},{2,0},{3,1},{4,6},{5,7},{6,4},{7,5},{8,10},{9,11},{10,... | collective-permute-start | bytes 1671176 | tf_op jit(solution)/shard_map/ppermute | solution.py:294
  5.8 19.0 %collective-permute-start.12 = (bf16[272,1024]{1,0:T(8,128)(2,1)S(1)}, bf16[272,1024]{1,0:T(8,128)(2,1)}, u32[]{:S(2)}, u32[]{:S(2)}) collective-permute-start(bf16[272,1024]{1,0:T(8,128)(2,1)S(1)} %normalise.1.refs_0_.refs_3_.refs_5_), channel_id=1, source_target_pairs={{8,0},{9,1},{10,2},{11,3},{12,4},{13,5},{14,6},{15,7},{16,8},{17,9... | collective-permute-start | bytes 1671176 | tf_op jit(solution)/shard_map/ppermute | solution.py:297
  7.1 18.1 %collective-permute-start.14 = (bf16[272,1024]{1,0:T(8,128)(2,1)S(1)}, bf16[272,1024]{1,0:T(8,128)(2,1)}, u32[]{:S(2)}, u32[]{:S(2)}) collective-permute-start(bf16[272,1024]{1,0:T(8,128)(2,1)S(1)} %normalise.1.refs_0_.refs_3_.refs_5_), channel_id=1, source_target_pairs={{0,8},{1,9},{2,10},{3,11},{4,12},{5,13},{6,14},{7,15},{8,16},{9,17... | collective-permute-start | bytes 1671176 | tf_op jit(solution)/shard_map/ppermute | solution.py:300
  12.5 13.0 %collective-permute-start.11 = (bf16[272,1024]{1,0:T(8,128)(2,1)S(1)}, bf16[272,1024]{1,0:T(8,128)(2,1)S(1)}, u32[]{:S(2)}, u32[]{:S(2)}) collective-permute-start(bf16[272,1024]{1,0:T(8,128)(2,1)S(1)} %normalise.1.refs_0_.refs_3_.refs_5_), channel_id=1, source_target_pairs={{0,1},{1,0},{2,3},{3,2},{4,5},{5,4},{6,7},{7,6},{8,9},{9,8},{10,11... | collective-permute-start | bytes 1671176 | tf_op jit(solution)/shard_map/ppermute | solution.py:294
  12.5 0.7 %copy-start = (s32[256]{0:T(256)S(1)}, s32[256]{0:T(256)}, u32[]{:S(2)}) copy-start(s32[256]{0:T(256)} %param.10) | copy-start | bytes 3076
  12.5 0.7 %copy-start.1 = (s32[32]{0:T(128)S(1)}, s32[32]{0:T(128)}, u32[]{:S(2)}) copy-start(s32[32]{0:T(128)} %param.11) | copy-start | bytes 388
  17.0 9.5 %collective-permute-start.10 = (bf16[144,1024]{1,0:T(8,128)(2,1)S(1)}, bf16[144,1024]{1,0:T(8,128)(2,1)S(1)}, u32[]{:S(2)}, u32[]{:S(2)}) collective-permute-start(bf16[144,1024]{1,0:T(8,128)(2,1)S(1)} %lower_half.1), channel_id=1, source_target_pairs={{0,2},{1,3},{2,0},{3,1},{4,6},{5,7},{6,4},{7,5},{8,10},{9,11},{10,... | collective-permute-start | bytes 884744 | tf_op jit(solution)/shard_map/ppermute | solution.py:294
  18.8 7.7 %collective-permute-start.9 = (bf16[128,1024]{1,0:T(8,128)(2,1)S(1)}, bf16[128,1024]{1,0:T(8,128)(2,1)S(1)}, u32[]{:S(2)}, u32[]{:S(2)}) collective-permute-start(bf16[128,1024]{1,0:T(8,128)(2,1)S(1)} %upper_half.1), channel_id=1, source_target_pairs={{0,4},{1,5},{2,6},{3,7},{4,0},{5,1},{6,2},{7,3},{8,12},{9,13},{10,... | collective-permute-start | bytes 786440 | tf_op jit(solution)/shard_map/ppermute | solution.py:294
  20.4 13.9 %all-to-all-start = ((f32[32,1,128]{2,1,0:T(1,128)}), f32[32,1,128]{2,1,0:T(1,128)S(1)}, u32[]{:S(2)}, u32[]{:S(2)}) async-start(f32[32,1,128]{2,1,0:T(1,128)} %message.1), calls=%async_computation | async-start | bytes 32768 | tf_op jit(solution)/shard_map/all_to_all | solution.py:318
  24.9 2.2 %collective-permute-start.13 = (bf16[272,1024]{1,0:T(8,128)(2,1)}, bf16[272,1024]{1,0:T(8,128)(2,1)S(1)}, u32[]{:S(2)}, u32[]{:S(2)}) collective-permute-start(bf16[272,1024]{1,0:T(8,128)(2,1)} %collective-permute-done.12.refs_7_), channel_id=1, source_target_pairs={{0,1},{1,0},{2,3},{3,2},{4,5},{5,4},{6,7},{7,6},{8,9},{9,8},{10,11... | collective-permute-start | bytes 1671176 | tf_op jit(solution)/shard_map/ppermute | solution.py:294
  25.2 2.7 %collective-permute-start.15 = (bf16[272,1024]{1,0:T(8,128)(2,1)}, bf16[272,1024]{1,0:T(8,128)(2,1)S(1)}, u32[]{:S(2)}, u32[]{:S(2)}) collective-permute-start(bf16[272,1024]{1,0:T(8,128)(2,1)} %collective-permute-done.14.refs_9_), channel_id=1, source_target_pairs={{0,1},{1,0},{2,3},{3,2},{4,5},{5,4},{6,7},{7,6},{8,9},{9,8},{10,11... | collective-permute-start | bytes 1671176 | tf_op jit(solution)/shard_map/ppermute | solution.py:294
  30.7 5.1 %collective-permute-start.17 = (f32[16,256]{1,0:T(8,128)S(1)}, f32[16,256]{1,0:T(8,128)S(1)}, u32[]{:S(2)}, u32[]{:S(2)}) collective-permute-start(f32[16,256]{1,0:T(8,128)S(1)} %get-tuple-element.114), channel_id=1, source_target_pairs={{0,4},{1,5},{2,6},{3,7},{4,0},{5,1},{6,2},{7,3},{8,12},{9,13},{10,... | collective-permute-start | bytes 49160 | tf_op jit(solution)/shard_map/ppermute | solution.py:294
  32.5 4.7 %collective-permute-start.18 = (f32[16,256]{1,0:T(8,128)S(1)}, f32[16,256]{1,0:T(8,128)S(1)}, u32[]{:S(2)}, u32[]{:S(2)}) collective-permute-start(f32[16,256]{1,0:T(8,128)S(1)} %get-tuple-element.115), channel_id=1, source_target_pairs={{0,6},{1,7},{2,4},{3,5},{4,2},{5,3},{6,0},{7,1},{8,14},{9,15},{10,... | collective-permute-start | bytes 49160 | tf_op jit(solution)/shard_map/ppermute | solution.py:294
  34.0 3.7 %collective-permute-start.16 = (f32[16,256]{1,0:T(8,128)S(1)}, f32[16,256]{1,0:T(8,128)S(1)}, u32[]{:S(2)}, u32[]{:S(2)}) collective-permute-start(f32[16,256]{1,0:T(8,128)S(1)} %get-tuple-element.113), channel_id=1, source_target_pairs={{0,2},{1,3},{2,0},{3,1},{4,6},{5,7},{6,4},{7,5},{8,10},{9,11},{10,... | collective-permute-start | bytes 49160 | tf_op jit(solution)/shard_map/ppermute | solution.py:294
  37.8 0.6 %copy-start.2 = (f32[256]{0:T(256)}, f32[256]{0:T(256)S(1)}, u32[]{:S(2)}) copy-start(f32[256]{0:T(256)S(1)} %get-tuple-element.276) | copy-start | bytes 3076

commit v3 on v2

--- a/solution.py
+++ b/solution.py
@@ -160,7 +160,7 @@
     )(*pieces)
 
 
-def tile_kernel(counts, n_right, places, rows, own_first, n_before, n_token, keep, *refs):
+def tile_kernel(counts, n_right, places, groups, rows, own_first, n_before, done, n_token, keep, *refs):
     parts, copies = [], []
     n_operands = sum(max(count, 1) for count in counts)
     tail = refs[n_operands + n_before + n_token :]
@@ -230,31 +230,26 @@
             row = places[c] + b
             outs[r][row : row + 1, :] = jnp.max(part, axis=0, keepdims=True)
 
-    for chip in range(0, len(places), 2):
-        todo = [
-            (r, c)
-            for c in range(chip, min(chip + 2, len(places)))
-            for r in range(n_right)
-            if r >= n_before or places[c] >= before[r].shape[0]
-        ]
+    for group in groups:
+        todo = [(r, c) for c in group for r in range(n_right) if r >= n_before or c not in done]
         meet = False
         for r, c in todo:
             right, left = labels_of(r), labels_of(n_right + c)
             meet |= (left[1] <= right[2]) & (right[1] <= left[2])
 
-        def chip_tiles(todo=todo):
+        def group_tiles(todo=todo):
             for r, c in todo:
                 tile(r, c)
 
-        if own_first:
-            chip_tiles()
+        if own_first and 0 in group:
+            group_tiles()
         else:
-            pl.when(meet)(chip_tiles)
+            pl.when(meet)(group_tiles)
     for copy in keeping.values():
         copy.wait()
 
 
-def tiles(name, rights, lefts, places, own_first, before=(), token=None, flops=None, keep=()):
+def tiles(name, rights, lefts, places, groups, own_first, before=(), done=(), token=None, flops=None, keep=()):
     parts = list(rights) + list(lefts)
     counts = tuple(len(part) if isinstance(part, list) else 0 for part in parts)
     operands = [piece for part in parts for piece in (part if isinstance(part, list) else [part])]
@@ -271,7 +266,7 @@
     if sum(counts) + len(keep):
         scratch.append(pltpu.SemaphoreType.DMA((sum(counts) + len(keep),)))
     return pl.pallas_call(
-        functools.partial(tile_kernel, counts, len(rights), tuple(places), rows, own_first, len(before), len(extra) - len(before), keep),
+        functools.partial(tile_kernel, counts, len(rights), tuple(places), groups, rows, own_first, len(before), done, len(extra) - len(before), keep),
         name=name,
         in_specs=specs + [vmem] * len(extra),
         out_specs=[vmem] * len(rights) + [pl.BlockSpec(memory_space=pltpu.HBM)] * len(keep),
@@ -317,19 +312,26 @@
 
     heard = lax.all_to_all(message, AXIS, split_axis=0, concat_axis=0, tiled=True)
 
-    plane_places = [0, blk_dev]
-    next_places = [8 + blk_dev * k for k in range(4)]
-    lefts = [[above], above_twin, [below], below_twin]
+    places = [0, blk_dev] + [8 + blk_dev * k for k in range(4)]
     near_rights = [unit, along_x, along_y]
-    plane_parts = tiles("plane_tiles", near_rights, [unit, twin], plane_places, True)
+    known = tiles(
+        "plane_tiles",
+        near_rights,
+        [unit, twin, [above], [below]],
+        [places[k] for k in (0, 1, 2, 4)],
+        ((0, 1), (2,), (3,)),
+        True,
+    )
     token = arrived(pieces)
     *parts, across = tiles(
         "all_tiles",
         near_rights + [pieces],
-        [unit, twin] + lefts,
-        plane_places + next_places,
+        [unit, twin, [above], above_twin, [below], below_twin],
+        places,
+        ((0, 1), (2, 3), (4, 5)),
         False,
-        plane_parts,
+        known,
+        (0, 1, 2, 4),
         token,
         flops=0,
         keep=(3,),
@@ -347,6 +349,7 @@
                 near_rights + [across],
                 lefts,
                 [blk_dev * k for k in range(4)],
+                ((0, 1), (2, 3)),
                 False,
             )
             cap, _ = cover(heard, offset, blk_dev, rows)

time: 38.6 us -> 37.3 us (0.966)
  waiting for transfers between devices: 6.21 us -> 5.02 us
    ppermute x10, waiting for transfers between devices: 6.21 us -> 5.01 us  [swap(): return lax.ppermute(x, AXIS, [(i, i ^ bit) for i in range(n)])]
  transfers between devices with their start and end apart: 13 -> 13, of which waited for: 5 -> 4; matrix products, arithmetic and copies ran while one was open for 0% -> 0% of each run, Pallas kernels for 15% -> 15%
where the time goes in v3:
time: 37.3 us; the launch traced here: 37.1 us
  starting transfers between devices  23.2 us (62%)
  Pallas kernels  6.78 us (18%)
  waiting for transfers between devices  5.02 us (13%)
  local copies, waits for them, and re-layouts  1.24 us (3%)
  between operations  0.82 us (2%)
    ppermute x10, starting transfers between devices, swap(): return lax.ppermute(x, AXIS, [(i, i ^ bit) for i in range(n)])  12 us
    ppermute x1, starting transfers between devices, from_below(): return lax.ppermute(x, AXIS, [(i, i + PLANE) for i in range(n - PLANE)])  5.38 us
    ppermute x10, waiting for transfers between devices, swap(): return lax.ppermute(x, AXIS, [(i, i ^ bit) for i in range(n)])  5.01 us
    all_to_all x1, starting transfers between devices, local(): lax.all_to_all(message, AXIS, split_axis=0, concat_axis=0, tiled=True)  4.49 us
    pallas_call x2, Pallas kernels, tiles(): pl.pallas_call(functools.partial(tile_kernel, counts, len(rights), tuple(...  3.74 us
    ppermute x1, starting transfers between devices, from_above(): return lax.ppermute(x, AXIS, [(i + PLANE, i) for i in range(n - PLANE)])  1.28 us
    pallas_call x1, Pallas kernels, normalise(): pl.pallas_call(normalise_kernel, name='normalise', in_specs=[pl.BlockSpec...  1.26 us
    unnamed x10, local copies, waits for them, and re-layouts  1.24 us
  transfers between devices with their start and end apart: 13, of which 4 were waited for; matrix products, arithmetic and copies ran while one was open for 0% of the time, Pallas kernels for 15%

profile of v3, /device:TPU:0, one launch (start us, length us, event | category | flops | bytes accessed | tf_op | source)
XLA Modules:
  0.0 37.1 jit_solution(9137873682538644357)
XLA Ops:
  0.0 1.3 %normalise.1.refs_0_.refs_3_.refs_5_ = bf16[272,1024]{1,0:T(8,128)(2,1)S(1)} custom-call(bf16[256,1024]{1,0:T(8,128)(2,1)} %x_hbm.1, s32[1,256]{1,0:T(1,128)} %bitcast.24), custom_call_target="tpu_custom_call" | custom-call | tf_op jit(solution)/shard_map/normalise/pallas_call | solution.py:39
  1.3 0.0 copy-start.4
  1.3 3.0 %collective-permute-start.8 = (bf16[272,1024]{1,0:T(8,128)(2,1)S(1)}, bf16[272,1024]{1,0:T(8,128)(2,1)S(1)}, u32[]{:S(2)}, u32[]{:S(2)}) collective-permute-start(bf16[272,1024]{1,0:T(8,128)(2,1)S(1)} %normalise.1.refs_0_.refs_3_.refs_5_), channel_id=1, source_target_pairs={{0,4},{1,5},{2,6},{3,7},{4,0},{5,1},{6,2},{7,3},{8,12},{9,13},{10,... | collective-permute-start | bytes 1671176 | tf_op jit(solution)/shard_map/ppermute | solution.py:289
  4.3 1.5 %collective-permute-start.7 = (bf16[272,1024]{1,0:T(8,128)(2,1)S(1)}, bf16[272,1024]{1,0:T(8,128)(2,1)S(1)}, u32[]{:S(2)}, u32[]{:S(2)}) collective-permute-start(bf16[272,1024]{1,0:T(8,128)(2,1)S(1)} %normalise.1.refs_0_.refs_3_.refs_5_), channel_id=1, source_target_pairs={{0,2},{1,3},{2,0},{3,1},{4,6},{5,7},{6,4},{7,5},{8,10},{9,11},{10,... | collective-permute-start | bytes 1671176 | tf_op jit(solution)/shard_map/ppermute | solution.py:289
  5.8 1.3 %collective-permute-start.12 = (bf16[272,1024]{1,0:T(8,128)(2,1)S(1)}, bf16[272,1024]{1,0:T(8,128)(2,1)}, u32[]{:S(2)}, u32[]{:S(2)}) collective-permute-start(bf16[272,1024]{1,0:T(8,128)(2,1)S(1)} %normalise.1.refs_0_.refs_3_.refs_5_), channel_id=1, source_target_pairs={{8,0},{9,1},{10,2},{11,3},{12,4},{13,5},{14,6},{15,7},{16,8},{17,9... | collective-permute-start | bytes 1671176 | tf_op jit(solution)/shard_map/ppermute | solution.py:292
  7.1 5.4 %collective-permute-start.14 = (bf16[272,1024]{1,0:T(8,128)(2,1)S(1)}, bf16[272,1024]{1,0:T(8,128)(2,1)}, u32[]{:S(2)}, u32[]{:S(2)}) collective-permute-start(bf16[272,1024]{1,0:T(8,128)(2,1)S(1)} %normalise.1.refs_0_.refs_3_.refs_5_), channel_id=1, source_target_pairs={{0,8},{1,9},{2,10},{3,11},{4,12},{5,13},{6,14},{7,15},{8,16},{9,17... | collective-permute-start | bytes 1671176 | tf_op jit(solution)/shard_map/ppermute | solution.py:295
  12.5 0.0 collective-permute-start.11
  12.5 0.0 copy-start
  12.5 0.0 copy-start.1
  12.5 0.7 %copy-done = s32[256]{0:T(256)S(1)} copy-done((s32[256]{0:T(256)S(1)}, s32[256]{0:T(256)}, u32[]{:S(2)}) %copy-start) | copy-done | bytes 1048
  13.2 0.8 %message.1 = f32[32,1,128]{2,1,0:T(1,128)} custom-call(s32[1,384]{1,0:T(1,128)S(1)} %reshape.16.left_ref, s32[1,384]{1,0:T(1,128)S(1)} %reshape.17.right_ref, s32[1,32]{1,0:T(1,128)S(1)} %bitcast.26, s32[1,256]{1,0:T(1,128)S(1)} %bitcast.25), custom_call_target="tpu_custom_call" | custom-call | tf_op jit(solution)/shard_map/message/pallas_call | solution.py:72
  14.0 2.9 %collective-permute-done.8.x_ref.refs_2_ = bf16[272,1024]{1,0:T(8,128)(2,1)S(1)} collective-permute-done((bf16[272,1024]{1,0:T(8,128)(2,1)S(1)}, bf16[272,1024]{1,0:T(8,128)(2,1)S(1)}, u32[]{:S(2)}, u32[]{:S(2)}) %collective-permute-start.8) | collective-permute-done | bytes 557088 | tf_op jit(solution)/shard_map/ppermute | solution.py:289
  17.0 1.8 %collective-permute-start.10 = (bf16[144,1024]{1,0:T(8,128)(2,1)S(1)}, bf16[144,1024]{1,0:T(8,128)(2,1)S(1)}, u32[]{:S(2)}, u32[]{:S(2)}) collective-permute-start(bf16[144,1024]{1,0:T(8,128)(2,1)S(1)} %lower_half.1), channel_id=1, source_target_pairs={{0,2},{1,3},{2,0},{3,1},{4,6},{5,7},{6,4},{7,5},{8,10},{9,11},{10,... | collective-permute-start | bytes 884744 | tf_op jit(solution)/shard_map/ppermute | solution.py:289
  18.7 0.0 collective-permute-done.7.x_ref.refs_1_
  18.8 1.6 %collective-permute-start.9 = (bf16[128,1024]{1,0:T(8,128)(2,1)S(1)}, bf16[128,1024]{1,0:T(8,128)(2,1)S(1)}, u32[]{:S(2)}, u32[]{:S(2)}) collective-permute-start(bf16[128,1024]{1,0:T(8,128)(2,1)S(1)} %upper_half.1), channel_id=1, source_target_pairs={{0,4},{1,5},{2,6},{3,7},{4,0},{5,1},{6,2},{7,3},{8,12},{9,13},{10,... | collective-permute-start | bytes 786440 | tf_op jit(solution)/shard_map/ppermute | solution.py:289
  20.4 4.5 %all-to-all-start = ((f32[32,1,128]{2,1,0:T(1,128)}), f32[32,1,128]{2,1,0:T(1,128)S(1)}, u32[]{:S(2)}, u32[]{:S(2)}) async-start(f32[32,1,128]{2,1,0:T(1,128)} %message.1), calls=%async_computation | async-start | bytes 32768 | tf_op jit(solution)/shard_map/all_to_all | solution.py:313
  24.9 0.0 collective-permute-done.12.refs_5_.refs_7_
  24.9 0.3 collective-permute-start.13
  25.2 0.3 collective-permute-start.15
  25.4 2.2 %plane_tiles.1 = (f32[16,256]{1,0:T(8,128)S(1)}, f32[16,256]{1,0:T(8,128)S(1)}, f32[16,256]{1,0:T(8,128)S(1)}) custom-call(bf16[272,1024]{1,0:T(8,128)(2,1)S(1)} %normalise.1.refs_0_.refs_3_.refs_5_, bf16[272,1024]{1,0:T(8,128)(2,1)S(1)} %collective-permute-done.7.x_ref.refs_1_, bf16[272,1024]{1,0:T(8,128)(2,1)S(1)} %collective-permute-done.8.x_ref.refs_2_, ...), custom_call_target="tpu_custom_call" | custom-call | flops 1610612736 | bytes 3670016 | tf_op jit(solution)/shard_map/plane_tiles/pallas_call | solution.py:268
  27.7 0.0 collective-permute-done.10.second_ref.refs_4_
  27.7 0.2 collective-permute-done.15.refs_10_
  27.9 1.5 %all_tiles.1 = (f32[16,256]{1,0:T(8,128)S(1)}, f32[16,256]{1,0:T(8,128)S(1)}, f32[16,256]{1,0:T(8,128)S(1)}, f32[16,256]{1,0:T(8,128)S(1)}, bf16[272,1024]{1,0:T(8,128)(2,1)S(1)}) custom-call(bf16[272,1024]{1,0:T(8,128)(2,1)S(1)} %normalise.1.refs_0_.refs_3_.refs_5_, bf16[272,1024]{1,0:T(8,128)(2,1)S(1)} %collective-permute-done.7.x_ref.refs_1_, ...), custom_call_target="tpu_custom_call" | custom-call | bytes 5767168 | tf_op jit(solution)/shard_map/all_tiles/pallas_call | solution.py:268
  29.4 1.8 %collective-permute-start.17 = (f32[16,256]{1,0:T(8,128)S(1)}, f32[16,256]{1,0:T(8,128)S(1)}, u32[]{:S(2)}, u32[]{:S(2)}) collective-permute-start(f32[16,256]{1,0:T(8,128)S(1)} %get-tuple-element.114), channel_id=1, source_target_pairs={{0,4},{1,5},{2,6},{3,7},{4,0},{5,1},{6,2},{7,3},{8,12},{9,13},{10,... | collective-permute-start | bytes 49160 | tf_op jit(solution)/shard_map/ppermute | solution.py:289
  31.3 1.5 %collective-permute-start.18 = (f32[16,256]{1,0:T(8,128)S(1)}, f32[16,256]{1,0:T(8,128)S(1)}, u32[]{:S(2)}, u32[]{:S(2)}) collective-permute-start(f32[16,256]{1,0:T(8,128)S(1)} %get-tuple-element.115), channel_id=1, source_target_pairs={{0,6},{1,7},{2,4},{3,5},{4,2},{5,3},{6,0},{7,1},{8,14},{9,15},{10,... | collective-permute-start | bytes 49160 | tf_op jit(solution)/shard_map/ppermute | solution.py:289
  32.7 0.3 collective-permute-start.16
  33.0 0.0 all-to-all-done.heard_ref
  33.0 0.9 %cover.2 = (f32[4,16,256]{2,1,0:T(8,128)S(1)}, s32[1]{0:T(128)}) custom-call(s32[1]{0:T(128)} %constant.4.clone.1.offset_ref, f32[32,1,128]{2,1,0:T(1,128)S(1)} %all-to-all-done.heard_ref), custom_call_target="tpu_custom_call" | custom-call | tf_op jit(solution)/shard_map/cover/pallas_call | solution.py:118
  34.5 1.4 %collective-permute-done.18 = f32[16,256]{1,0:T(8,128)S(1)} collective-permute-done((f32[16,256]{1,0:T(8,128)S(1)}, f32[16,256]{1,0:T(8,128)S(1)}, u32[]{:S(2)}, u32[]{:S(2)}) %collective-permute-start.18) | collective-permute-done | bytes 16416 | tf_op jit(solution)/shard_map/ppermute | solution.py:289
  36.0 0.5 %collective-permute-done.16 = f32[16,256]{1,0:T(8,128)S(1)} collective-permute-done((f32[16,256]{1,0:T(8,128)S(1)}, f32[16,256]{1,0:T(8,128)S(1)}, u32[]{:S(2)}, u32[]{:S(2)}) %collective-permute-start.16) | collective-permute-done | bytes 16416 | tf_op jit(solution)/shard_map/ppermute | solution.py:289
  36.5 0.0 copy-start.2
  36.5 0.6 %copy-done.2 = f32[256]{0:T(256)} copy-done((f32[256]{0:T(256)}, f32[256]{0:T(256)S(1)}, u32[]{:S(2)}) %copy-start.2) | copy-done | bytes 1048
  (17 shorter events, 0.1 us)
Async XLA Ops:
  0.0 12.5 %copy-start.3 = (s32[384]{0:T(512)S(1)}, s32[384]{0:T(512)}, u32[]{:S(2)}) copy-start(s32[384]{0:T(512)} %param.12) | copy-start | bytes 4612
  1.3 11.2 %copy-start.4 = (s32[384]{0:T(512)S(1)}, s32[384]{0:T(512)}, u32[]{:S(2)}) copy-start(s32[384]{0:T(512)} %param.13) | copy-start | bytes 4612
  1.3 15.7 %collective-permute-start.8 = (bf16[272,1024]{1,0:T(8,128)(2,1)S(1)}, bf16[272,1024]{1,0:T(8,128)(2,1)S(1)}, u32[]{:S(2)}, u32[]{:S(2)}) collective-permute-start(bf16[272,1024]{1,0:T(8,128)(2,1)S(1)} %normalise.1.refs_0_.refs_3_.refs_5_), channel_id=1, source_target_pairs={{0,4},{1,5},{2,6},{3,7},{4,0},{5,1},{6,2},{7,3},{8,12},{9,13},{10,... | collective-permute-start | bytes 1671176 | tf_op jit(solution)/shard_map/ppermute | solution.py:289
  4.3 14.4 %collective-permute-start.7 = (bf16[272,1024]{1,0:T(8,128)(2,1)S(1)}, bf16[272,1024]{1,0:T(8,128)(2,1)S(1)}, u32[]{:S(2)}, u32[]{:S(2)}) collective-permute-start(bf16[272,1024]{1,0:T(8,128)(2,1)S(1)} %normalise.1.refs_0_.refs_3_.refs_5_), channel_id=1, source_target_pairs={{0,2},{1,3},{2,0},{3,1},{4,6},{5,7},{6,4},{7,5},{8,10},{9,11},{10,... | collective-permute-start | bytes 1671176 | tf_op jit(solution)/shard_map/ppermute | solution.py:289
  5.8 19.0 %collective-permute-start.12 = (bf16[272,1024]{1,0:T(8,128)(2,1)S(1)}, bf16[272,1024]{1,0:T(8,128)(2,1)}, u32[]{:S(2)}, u32[]{:S(2)}) collective-permute-start(bf16[272,1024]{1,0:T(8,128)(2,1)S(1)} %normalise.1.refs_0_.refs_3_.refs_5_), channel_id=1, source_target_pairs={{8,0},{9,1},{10,2},{11,3},{12,4},{13,5},{14,6},{15,7},{16,8},{17,9... | collective-permute-start | bytes 1671176 | tf_op jit(solution)/shard_map/ppermute | solution.py:292
  7.1 18.1 %collective-permute-start.14 = (bf16[272,1024]{1,0:T(8,128)(2,1)S(1)}, bf16[272,1024]{1,0:T(8,128)(2,1)}, u32[]{:S(2)}, u32[]{:S(2)}) collective-permute-start(bf16[272,1024]{1,0:T(8,128)(2,1)S(1)} %normalise.1.refs_0_.refs_3_.refs_5_), channel_id=1, source_target_pairs={{0,8},{1,9},{2,10},{3,11},{4,12},{5,13},{6,14},{7,15},{8,16},{9,17... | collective-permute-start | bytes 1671176 | tf_op jit(solution)/shard_map/ppermute | solution.py:295
  12.5 13.0 %collective-permute-start.11 = (bf16[272,1024]{1,0:T(8,128)(2,1)S(1)}, bf16[272,1024]{1,0:T(8,128)(2,1)S(1)}, u32[]{:S(2)}, u32[]{:S(2)}) collective-permute-start(bf16[272,1024]{1,0:T(8,128)(2,1)S(1)} %normalise.1.refs_0_.refs_3_.refs_5_), channel_id=1, source_target_pairs={{0,1},{1,0},{2,3},{3,2},{4,5},{5,4},{6,7},{7,6},{8,9},{9,8},{10,11... | collective-permute-start | bytes 1671176 | tf_op jit(solution)/shard_map/ppermute | solution.py:289
  12.5 0.7 %copy-start = (s32[256]{0:T(256)S(1)}, s32[256]{0:T(256)}, u32[]{:S(2)}) copy-start(s32[256]{0:T(256)} %param.10) | copy-start | bytes 3076
  12.5 0.7 %copy-start.1 = (s32[32]{0:T(128)S(1)}, s32[32]{0:T(128)}, u32[]{:S(2)}) copy-start(s32[32]{0:T(128)} %param.11) | copy-start | bytes 388
  17.0 10.7 %collective-permute-start.10 = (bf16[144,1024]{1,0:T(8,128)(2,1)S(1)}, bf16[144,1024]{1,0:T(8,128)(2,1)S(1)}, u32[]{:S(2)}, u32[]{:S(2)}) collective-permute-start(bf16[144,1024]{1,0:T(8,128)(2,1)S(1)} %lower_half.1), channel_id=1, source_target_pairs={{0,2},{1,3},{2,0},{3,1},{4,6},{5,7},{6,4},{7,5},{8,10},{9,11},{10,... | collective-permute-start | bytes 884744 | tf_op jit(solution)/shard_map/ppermute | solution.py:289
  18.8 8.9 %collective-permute-start.9 = (bf16[128,1024]{1,0:T(8,128)(2,1)S(1)}, bf16[128,1024]{1,0:T(8,128)(2,1)S(1)}, u32[]{:S(2)}, u32[]{:S(2)}) collective-permute-start(bf16[128,1024]{1,0:T(8,128)(2,1)S(1)} %upper_half.1), channel_id=1, source_target_pairs={{0,4},{1,5},{2,6},{3,7},{4,0},{5,1},{6,2},{7,3},{8,12},{9,13},{10,... | collective-permute-start | bytes 786440 | tf_op jit(solution)/shard_map/ppermute | solution.py:289
  20.4 12.6 %all-to-all-start = ((f32[32,1,128]{2,1,0:T(1,128)}), f32[32,1,128]{2,1,0:T(1,128)S(1)}, u32[]{:S(2)}, u32[]{:S(2)}) async-start(f32[32,1,128]{2,1,0:T(1,128)} %message.1), calls=%async_computation | async-start | bytes 32768 | tf_op jit(solution)/shard_map/all_to_all | solution.py:313
  24.9 2.9 %collective-permute-start.13 = (bf16[272,1024]{1,0:T(8,128)(2,1)}, bf16[272,1024]{1,0:T(8,128)(2,1)S(1)}, u32[]{:S(2)}, u32[]{:S(2)}) collective-permute-start(bf16[272,1024]{1,0:T(8,128)(2,1)} %collective-permute-done.12.refs_5_.refs_7_), channel_id=1, source_target_pairs={{0,1},{1,0},{2,3},{3,2},{4,5},{5,4},{6,7},{7,6},{8,9},{9,8},{10,11... | collective-permute-start | bytes 1671176 | tf_op jit(solution)/shard_map/ppermute | solution.py:289
  25.2 2.7 %collective-permute-start.15 = (bf16[272,1024]{1,0:T(8,128)(2,1)}, bf16[272,1024]{1,0:T(8,128)(2,1)S(1)}, u32[]{:S(2)}, u32[]{:S(2)}) collective-permute-start(bf16[272,1024]{1,0:T(8,128)(2,1)} %collective-permute-done.14.refs_6_.refs_9_), channel_id=1, source_target_pairs={{0,1},{1,0},{2,3},{3,2},{4,5},{5,4},{6,7},{7,6},{8,9},{9,8},{10,11... | collective-permute-start | bytes 1671176 | tf_op jit(solution)/shard_map/ppermute | solution.py:289
  29.4 5.1 %collective-permute-start.17 = (f32[16,256]{1,0:T(8,128)S(1)}, f32[16,256]{1,0:T(8,128)S(1)}, u32[]{:S(2)}, u32[]{:S(2)}) collective-permute-start(f32[16,256]{1,0:T(8,128)S(1)} %get-tuple-element.114), channel_id=1, source_target_pairs={{0,4},{1,5},{2,6},{3,7},{4,0},{5,1},{6,2},{7,3},{8,12},{9,13},{10,... | collective-permute-start | bytes 49160 | tf_op jit(solution)/shard_map/ppermute | solution.py:289
  31.3 4.7 %collective-permute-start.18 = (f32[16,256]{1,0:T(8,128)S(1)}, f32[16,256]{1,0:T(8,128)S(1)}, u32[]{:S(2)}, u32[]{:S(2)}) collective-permute-start(f32[16,256]{1,0:T(8,128)S(1)} %get-tuple-element.115), channel_id=1, source_target_pairs={{0,6},{1,7},{2,4},{3,5},{4,2},{5,3},{6,0},{7,1},{8,14},{9,15},{10,... | collective-permute-start | bytes 49160 | tf_op jit(solution)/shard_map/ppermute | solution.py:289
  32.7 3.7 %collective-permute-start.16 = (f32[16,256]{1,0:T(8,128)S(1)}, f32[16,256]{1,0:T(8,128)S(1)}, u32[]{:S(2)}, u32[]{:S(2)}) collective-permute-start(f32[16,256]{1,0:T(8,128)S(1)} %get-tuple-element.113), channel_id=1, source_target_pairs={{0,2},{1,3},{2,0},{3,1},{4,6},{5,7},{6,4},{7,5},{8,10},{9,11},{10,... | collective-permute-start | bytes 49160 | tf_op jit(solution)/shard_map/ppermute | solution.py:289
  36.5 0.6 %copy-start.2 = (f32[256]{0:T(256)}, f32[256]{0:T(256)S(1)}, u32[]{:S(2)}) copy-start(f32[256]{0:T(256)S(1)} %get-tuple-element.276) | copy-start | bytes 3076
